TPU v7x, 32 devices: a whole 2x2x4 slice. The times are simulated.
32 devices in a mesh: section: 4 (over y, x), dp: 8 (over z, core).
Axes of the slice: x: 2, y: 2, z: 4, core: 2. Of those that a mesh axis runs over, the one named last changes fastest.
Arguments:
- inputs: bfloat16 [61440, 512], P('dp'), may hold values from -6 to 6
- cotangent: bfloat16 [61440, 512], P('dp'), may hold values from -6 to 6
- latent_codes: bfloat16 [64, 256], replicated, may hold values from -6 to 6
- positions: bfloat16 [3, 61440], P(None, 'dp'), may hold values from -1 to 1
- shape_ids: int32 [61440], P('dp'), may hold values from 0 to 63
- direction_first: bfloat16 [4, 771, 512], P('section'), may hold values from -0.21875 to 0.21875
- gain_first: bfloat16 [4, 512], P('section'), may hold values from 0.099609375 to 1.8984375
- bias_first: bfloat16 [4, 512], P('section'), may hold values from -3 to 3
- direction_second: bfloat16 [4, 512, 512], P('section'), may hold values from -0.25 to 0.25
- gain_second: bfloat16 [4, 512], P('section'), may hold values from 0.099609375 to 1.8984375
- bias_second: bfloat16 [4, 512], P('section'), may hold values from -3 to 3
Outputs:
- activations: bfloat16 [4, 61440, 512], P('section', 'dp')
- input_grads: bfloat16 [4, 61440, 512], P('section', 'dp')
- code_grad: float32 [64, 256], P(('section', 'dp'))
- direction_first_grad: float32 [4, 771, 512], P('section')
- gain_first_grad: float32 [4, 512], P('section')
- bias_first_grad: float32 [4, 512], P('section')
- direction_second_grad: float32 [4, 512, 512], P('section')
- gain_second_grad: float32 [4, 512], P('section')
- bias_second_grad: float32 [4, 512], P('section')
All inputs are finite; a program needn't handle non-finite values.
Results may differ from a plain program's by a relative error of at most 0.0095.
Values may be sent and summed in bfloat16 or wider, within the bound.
No kernel may reach another device: no remote copies, remote signals or barrier semaphores. Data moves between devices by JAX's collectives and lax.ppermute only.
A program may use at most 128 MiB of HBM per device.

v0:
```python
import functools

import jax
import jax.numpy as jnp
import numpy as np
from jax import lax
from jax.experimental import pallas as pl
from jax.experimental.pallas import tpu as pltpu
from jax.sharding import PartitionSpec as P

BF = jnp.bfloat16
F32 = jnp.float32
NT = (((1,), (1,)), ((), ()))
TN = (((0,), (0,)), ((), ()))
SECTIONS = 4
ROWS = 768
CALLS = (3, 2)
HELPED_CALLS = ((0,), (1,))
VMEM = 36 * 2**20
SMALL_VMEM = 12 * 2**20
ALL_VMEM = 63 * 2**20
GIVE_X = (7, 6, 3, 8)
GIVE_Y = (8, 3, 6, 7)


def up(value, step):
    return -(-value // step) * step


def mm(left, right, dims=(((1,), (0,)), ((), ()))):
    return lax.dot_general(left, right, dims, preferred_element_type=F32)


def silu_parts(half):
    lift = 1.0 + jnp.tanh(half)
    out = (half * lift).astype(BF)
    lift = lift.astype(BF)
    return out, lift + out * (BF(2.0) - lift)


def stream(count, *stages):
    values = [None] * count
    for tick in range(count + len(stages) - 1):
        for j, stage in enumerate(stages):
            i = tick - j
            if 0 <= i < count:
                values[i] = stage(i, values[i])


class Plan:
    def __init__(self, width, coords, shapes, devices):
        self.width, self.coords, self.shapes, self.devices = width, coords, shapes, devices
        self.spots = devices // 2
        self.share = width // devices
        self.owned = shapes // devices
        self.per = self.owned // SECTIONS
        self.room = up(self.owned + 1, 16)
        self.cells = self.room * devices
        self.piece = 2 * self.share + self.room
        self.half = self.piece * self.spots
        self.packed = 2 * self.half
        table = np.full((self.cells, 1), -1, np.int32)
        for p in range(devices):
            place = 2 * (p % self.spots) + p // self.spots
            for j in range(self.owned):
                table[p * self.room + j, 0] = ((j // self.per) * devices + place) * self.per + j % self.per
        self.cell_shape = table

    def grant(self, base):
        return base + max(0, self.cells - 128) * 12288

    def special(self, j):
        return j * self.room + self.owned


class Block:
    def __init__(self, plan, weights, ext, subs):
        self.width, self.plan, self.weights, self.ext, self.subs = plan.width, plan, weights, ext, subs

    def first(self, k):
        return self.weights[k, : self.width, :]

    def second(self, k):
        return self.weights[k, self.width : 2 * self.width, :]

    def inner(self, k, source):
        beside = self.weights[k, 2 * self.width :, :]
        return lambda i, unused: mm(source(i), self.first(k)) + mm(self.ext[self.subs[i], :], beside)

    def outer(self, k):
        begin = 2 * self.width + self.plan.coords * self.plan.room
        spot = self.plan.owned
        offset = self.weights[k, begin : begin + self.plan.room, :].astype(F32)[spot : spot + 1]
        return lambda i, active: mm(active, self.second(k)) + offset

    def back_second(self, k, grads):
        return lambda i, unused: mm(grads(i), self.second(k), NT)

    def back_first(self, k):
        return lambda i, grads: mm(grads, self.first(k), NT)


def place_cells(point, places, cell_shape, plan, ext, ext_turned):
    rows = ext.shape[0]
    hit = jnp.where(cell_shape[...] == jnp.broadcast_to(point[...], (plan.cells, rows)), 1.0, 0.0)
    cell = lax.broadcasted_iota(jnp.int32, (plan.cells, rows), 0)
    for j in range(plan.coords):
        hit = jnp.where(cell == plan.special(j), places[j : j + 1, :].astype(F32), hit)
    ext_turned[...] = hit.astype(BF)
    ext[...] = hit.T.astype(BF)


def add_weight_grads(accs, active, outer_grad, entering, inner_grad, ext_turned):
    first, second, cell, bias = accs
    second[...] += mm(active, outer_grad, TN)
    first[...] += mm(entering, inner_grad, TN)
    cell[...] += mm(ext_turned[...], inner_grad)
    bias[...] += jnp.sum(outer_grad.astype(F32).reshape(-1, 8, outer_grad.shape[1]), axis=0)


def store_weight_grads(accs, plan, core, mine, theirs):
    first, second, cell, bias = accs
    share, room = plan.share, plan.room
    last = jnp.sum(bias[...], axis=0, keepdims=True)
    row = lax.broadcasted_iota(jnp.int32, cell.shape, 0)
    cell[...] = jnp.where(row == plan.special(plan.coords), last, cell[...])
    for side in range(2):
        @pl.when(core == side)
        def _(side=side):
            for p in range(plan.devices):
                out = mine if p // plan.spots == side else theirs
                at = (p % plan.spots) * plan.piece
                out[at : at + share, :] = second[p * share : (p + 1) * share, :].astype(BF)
                out[at + share : at + 2 * share, :] = first[p * share : (p + 1) * share, :].astype(BF)
                out[at + 2 * share : at + plan.piece, :] = cell[p * room : (p + 1) * room, :].astype(BF)


def pick(section, choices):
    found = jnp.int32(choices[0])
    for k in range(1, SECTIONS):
        found = jnp.where(section == k, choices[k], found)
    return found


def self_half(section, blocks):
    return jnp.where((section == 0) | (section == SECTIONS - 1), 0, blocks // 2)


def self_kernel(
    plan, steps, aliased, sc, h_in, g_in, ids, places, other_h, other_ids, other_places, cell_shape, weights, *refs
):
    act, ig, give_x, give_y, after_first, mine, theirs, ext, ext_turned, states, mids, slope1, slope2, *accs = refs[aliased:]
    section, core = sc[0], sc[1]
    step = pl.program_id(0)
    rows = h_in.shape[0]
    half = rows // 2
    subs = [pl.ds(0, half), pl.ds(half, half)]
    do = Block(plan, weights, ext, subs)

    @pl.when(step == 0)
    def _():
        for acc in accs:
            acc[...] = jnp.zeros_like(acc)

    @pl.when(section == 2)
    def _():
        place_cells(other_ids, other_places, cell_shape, plan, ext, ext_turned)

        def keep(i, z):
            after_first[pl.ds(pl.multiple_of(step * rows + i * half, 128), half), :] = silu_parts(z)[0]
        stream(2, do.inner(0, lambda i: other_h[subs[i], :]), lambda i, z: silu_parts(z)[0], do.outer(0), keep)

    place_cells(ids, places, cell_shape, plan, ext, ext_turned)
    states[0] = h_in[...]

    def keep_active(k):
        def stage(i, z):
            active, slope = silu_parts(z)
            mids[k, subs[i], :] = active
            slope1[k, subs[i], :] = slope
            return active
        return stage

    def keep_state(k):
        def stage(i, z):
            after, slope = silu_parts(z)
            states[k + 1, subs[i], :] = after
            if k == SECTIONS - 1:
                slope = slope * (g_in[subs[i], :] * BF(0.5))
            slope2[k, subs[i], :] = slope
        return stage

    def inner_grad(k):
        def stage(i, grads):
            grads = (grads * slope1[k, subs[i], :].astype(F32)).astype(BF)
            slope1[k, subs[i], :] = grads
            return grads
        return stage

    def enter_grad(k, below):
        def stage(i, grads):
            grads = grads.astype(BF)
            states[5 + k, subs[i], :] = grads
            if below is not None:
                slope2[below, subs[i], :] = grads * slope2[below, subs[i], :]
        return stage

    def back(k, below):
        return [do.back_second(k, lambda i: slope2[k, subs[i], :]), inner_grad(k), do.back_first(k),
                enter_grad(k, below)]

    top = SECTIONS - 1
    stages = []
    for k in range(SECTIONS):
        source = (lambda i: h_in[subs[i], :]) if k == 0 else (lambda i, k=k: states[k, subs[i], :])
        stages += [do.inner(k, source), keep_active(k), do.outer(k), keep_state(k)]
    stream(2, *stages, *back(top, top - 1))

    def lower(j, unused):
        k = top - 1 - j
        stream(2, *back(k, jnp.where(k > 0, k - 1, SECTIONS)))
        return 0

    lax.fori_loop(0, top - section, lower, 0)

    @pl.when(section >= 2)
    def _():
        value = None
        for stage in back(section - 1, None):
            value = stage(1, value)

    act[...] = states[section + 1]
    ig[...] = states[5 + section] * BF(2.0)
    given = pl.ds(pl.multiple_of(step * half, 128), half)
    give_x[given, :] = states[pick(section, GIVE_X), subs[0], :]
    give_y[given, :] = states[pick(section, GIVE_Y), subs[1], :]
    add_weight_grads(accs, mids[section], slope2[section], states[section], slope1[section], ext_turned)

    @pl.when(step == steps - 1)
    def _():
        store_weight_grads(accs, plan, core, mine, theirs)


def helped_kernel(
    plan, steps, counts, sc, h_in, g_in, ids, places, cell_shape, weights, *refs
):
    sources, refs = refs[: 3 * len(counts)], refs[3 * len(counts) + 2 :]
    act, ig, mine, theirs, ext, ext_turned, entering, got, mid, slope1, slope2, *accs = refs
    section, core = sc[0], sc[1]
    step = pl.program_id(0)
    rows = h_in.shape[0]
    half = rows // 2
    subs = [pl.ds(0, half), pl.ds(half, half)]
    do = Block(plan, weights, ext, subs)

    @pl.when(step == 0)
    def _():
        for acc in accs:
            acc[...] = jnp.zeros_like(acc)

    place_cells(ids, places, cell_shape, plan, ext, ext_turned)
    top = section == SECTIONS - 1
    begin = 0
    for j, count in enumerate(counts):
        got_x, got_y, after_first = sources[3 * j : 3 * j + 3]
        now = (step >= begin) & (step < begin + count)
        begin += count

        @pl.when(now)
        def _():
            got[subs[0], :] = got_x[...]
            got[subs[1], :] = got_y[...]

        @pl.when(now & (section == 2))
        def _():
            entering[...] = after_first[...]

    @pl.when(section <= 1)
    def _():
        entering[...] = h_in[...]

    @pl.when(top)
    def _():
        entering[...] = got[...]
        got[...] = g_in[...] * BF(0.5)

    def active_only(i, z):
        return silu_parts(z)[0]

    def enter(i, z):
        entering[subs[i], :] = silu_parts(z)[0]

    def keep_active(i, z):
        active, slope = silu_parts(z)
        mid[subs[i], :] = active
        slope1[subs[i], :] = slope
        return active

    def keep_own(i, z):
        after, slope = silu_parts(z)
        act[subs[i], :] = after
        grads = slope * got[subs[i], :]
        slope2[subs[i], :] = grads
        return grads

    def inner_grad(i, grads):
        grads = (grads * slope1[subs[i], :].astype(F32)).astype(BF)
        slope1[subs[i], :] = grads
        return grads

    def enter_grad(i, grads):
        ig[subs[i], :] = (2.0 * grads).astype(BF)

    def source(i):
        return entering[subs[i], :]

    @pl.when((section == 1) | (section == 2))
    def _():
        stream(2, do.inner(section - 1, source), active_only, do.outer(section - 1), enter)

    stream(2, do.inner(section, source), keep_active, do.outer(section), keep_own,
           do.back_second(section, lambda i: slope2[subs[i], :]), inner_grad, do.back_first(section), enter_grad)
    add_weight_grads(accs, mid[...], slope2[...], entering[...], slope1[...], ext_turned)

    @pl.when(step == steps - 1)
    def _():
        store_weight_grads(accs, plan, core, mine, theirs)


def run_blocks(plan, done, place, h, g, ids, places, cell_shape, weights, into, counts, sources):
    total, width = h.shape
    blocks = total // ROWS
    helped = len(sources) > 0
    steps = sum(counts)

    def here(i, sc):
        start = self_half(sc[0], blocks)
        return (blocks // 2 - start if helped else start) + done + i

    def there(i, sc):
        return jnp.where(sc[0] == 2, blocks // 2 - self_half(sc[0], blocks) + done + i, 0)

    def block_specs(where):
        return [
            pl.BlockSpec((None, 1, ROWS), lambda i, sc: (where(i, sc), 0, 0)),
            pl.BlockSpec((None, plan.coords, ROWS), lambda i, sc: (where(i, sc), 0, 0)),
        ]

    rows = pl.BlockSpec((ROWS, width), lambda i, sc: (here(i, sc), 0))
    other_rows = pl.BlockSpec((ROWS, width), lambda i, sc: (there(i, sc), 0))
    hbm = pl.BlockSpec(memory_space=pl.ANY)
    vmem = pl.BlockSpec(memory_space=pltpu.VMEM)
    array = lambda count: jax.ShapeDtypeStruct((count, width), BF)
    block = lambda *lead: pltpu.VMEM((*lead, ROWS, width), BF)
    scratch = [pltpu.VMEM((ROWS, plan.cells), BF), pltpu.VMEM((plan.cells, ROWS), BF)]
    if helped:
        kernel = functools.partial(helped_kernel, plan, steps, counts)
        out_shape = [array(total)] * 2 + [array(plan.half)] * 2
        out_specs = [rows, rows, vmem, vmem]
        scratch += [block()] * 5
        source_specs, begin = [], 0
        for count in counts:
            at = lambda i, sc, begin=begin, count=count: (jnp.clip(i - begin, 0, count - 1), 0)
            half_rows = pl.BlockSpec((ROWS // 2, width), at)
            source_specs += [half_rows, half_rows, pl.BlockSpec((ROWS, width), at)]
            begin += count
        operands = [h, g, ids, places, cell_shape, weights, *sources, *into]
        in_specs = [rows, rows, *block_specs(here), vmem, vmem, *source_specs, hbm, hbm]
        units = 8
    else:
        kernel = functools.partial(self_kernel, plan, steps, len(into))
        out_shape = ([array(total)] * 2 + [array(steps * ROWS // 2)] * 2 + [array(steps * ROWS)]
                     + [array(plan.half)] * 2)
        out_specs = [rows, rows, *[vmem] * 5]
        scratch += [block(10), block(SECTIONS), block(SECTIONS), block(SECTIONS + 1)]
        operands = [h, g, ids, places, h, ids, places, cell_shape, weights, *into]
        in_specs = [rows, rows, *block_specs(here), other_rows, *block_specs(there), vmem, vmem, *[hbm] * len(into)]
        units = 21
    scratch += [pltpu.VMEM((width, width), F32), pltpu.VMEM((width, width), F32),
                pltpu.VMEM((plan.cells, width), F32), pltpu.VMEM((8, width), F32)]
    first_into = 1 + len(operands) - len(into)
    return pl.pallas_call(
        kernel,
        grid_spec=pltpu.PrefetchScalarGridSpec(
            num_scalar_prefetch=1, grid=(steps,), in_specs=in_specs, out_specs=out_specs, scratch_shapes=scratch,
        ),
        out_shape=out_shape,
        input_output_aliases={first_into + j: j for j in range(len(into))},
        compiler_params=pltpu.CompilerParams(vmem_limit_bytes=plan.grant(VMEM)),
        cost_estimate=pl.CostEstimate(
            flops=2 * steps * ROWS * width * width * units, bytes_accessed=steps * ROWS * width * 12,
            transcendentals=steps * ROWS * width * 8,
        ),
    )(place, *operands)


def normed(direction, gain_row):
    scale = gain_row / jnp.sqrt(jnp.sum(direction * direction, axis=0, keepdims=True) + 1e-06)
    return (direction * scale).astype(BF)


def pack_kernel(plan, latent, *refs):
    sources, (packed, skip, side, far), held, sems = refs[:8], refs[8:12], refs[12:20], refs[20]
    copies = [pltpu.make_async_copy(s, h, sems.at[j]) for j, (s, h) in enumerate(zip(sources, held))]
    for copy in copies:
        copy.start()
    for copy in copies:
        copy.wait()
    dir_first, gain_first, bias_first, dir_second, gain_second, bias_second, latents, cell_shape = held
    width = plan.width
    half = BF(0.5)
    first = normed(dir_first[...].astype(F32), gain_first[...].astype(F32))
    second = normed(dir_second[...].astype(F32), gain_second[...].astype(F32))
    packed[:width, :] = first[:width] * half
    packed[width : 2 * width, :] = second * half
    skip[...] = first[width : width + latent]
    shape = lax.broadcasted_iota(jnp.int32, (plan.cells, plan.shapes), 1)
    onehot = jnp.where(cell_shape[...] == shape, 1.0, 0.0).astype(BF)
    by_cell = mm(onehot, latents[...]).astype(BF)
    by_cell = mm(by_cell, skip[...])
    by_cell = 0.5 * jnp.where(cell_shape[...] >= 0, by_cell + bias_first[...].astype(F32), 0.0)
    cell = lax.broadcasted_iota(jnp.int32, by_cell.shape, 0)
    tail = 0.5 * first[width + latent :].astype(F32)
    for j in range(plan.coords):
        by_cell = jnp.where(cell == plan.special(j), tail[j : j + 1], by_cell)
    by_cell = jnp.where(cell == plan.special(plan.coords), 0.5 * bias_second[...].astype(F32), by_cell)
    packed[2 * width :, :] = by_cell.astype(BF)
    place = lax.axis_index("dp")
    begin = lax.rem(place, 2) * plan.half
    side[...] = packed[pl.ds(pl.multiple_of(begin, 16), plan.half), :]
    far[...] = packed[pl.ds(pl.multiple_of(begin + lax.div(place, 2) * plan.piece, 16), plan.piece), :]


def pack_weights(plan, latents, cell_shape, *own):
    width = plan.width
    latent = latents.shape[1]
    vmem = pl.BlockSpec(memory_space=pltpu.VMEM)
    return pl.pallas_call(
        functools.partial(pack_kernel, plan, latent),
        in_specs=[pl.BlockSpec(memory_space=pl.ANY)] * 8,
        out_specs=[vmem] * 4,
        scratch_shapes=[pltpu.VMEM(array.shape, array.dtype) for array in (*own, latents, cell_shape)]
        + [pltpu.SemaphoreType.DMA((8,))],
        out_shape=[jax.ShapeDtypeStruct((rows, width), BF) for rows in (plan.packed, latent, plan.half, plan.piece)],
        compiler_params=pltpu.CompilerParams(vmem_limit_bytes=ALL_VMEM),
        cost_estimate=pl.CostEstimate(flops=2 * plan.cells * width * latent, bytes_accessed=4 * plan.packed * width,
                                      transcendentals=0),
    )(*own, latents, cell_shape)


def join_kernel(count, *refs):
    sources, out, sems = refs[:count], refs[count], refs[count + 1]
    copies, row = [], 0
    for j, source in enumerate(sources):
        copies.append(pltpu.make_async_copy(source, out.at[pl.ds(row, source.shape[0])], sems.at[j]))
        row += source.shape[0]
    for copy in copies:
        copy.start()
    for copy in copies:
        copy.wait()


def join(plan, arrays):
    rows = sum(array.shape[0] for array in arrays)
    return pl.pallas_call(
        functools.partial(join_kernel, len(arrays)),
        in_specs=[pl.BlockSpec(memory_space=pl.ANY)] * len(arrays),
        out_specs=pl.BlockSpec(memory_space=pltpu.VMEM),
        scratch_shapes=[pltpu.SemaphoreType.DMA((len(arrays),))],
        out_shape=jax.ShapeDtypeStruct((rows, arrays[0].shape[1]), arrays[0].dtype),
        compiler_params=pltpu.CompilerParams(vmem_limit_bytes=plan.grant(SMALL_VMEM)),
        cost_estimate=pl.CostEstimate(flops=0, bytes_accessed=4 * rows * arrays[0].shape[1], transcendentals=0),
    )(*arrays)


def spread_kernel(plan, sc, own, mine, other, weights, sems):
    section, core, spot = sc[0], sc[1], sc[2]
    half, piece = plan.half, plan.piece
    away = 1 - core
    copies = [(own, weights.at[section])]
    for j in range(2):
        there = weights.at[jnp.bitwise_xor(section, j + 1)]
        for block, side in ((mine, core), (other, away)):
            copies.append((block.at[pl.ds(j * half, half)], there.at[pl.ds(side * half, half)]))
    there = weights.at[jnp.bitwise_xor(section, 3)]
    for j in range(plan.spots):
        z = jnp.bitwise_xor(spot, j)
        for block, side in ((mine, core), (other, away)):
            copies.append((block.at[pl.ds(2 * half + j * piece, piece)], there.at[pl.ds(side * half + z * piece, piece)]))
    copies = [pltpu.make_async_copy(source, target, sems.at[j]) for j, (source, target) in enumerate(copies)]
    for copy in copies:
        copy.start()
    for copy in copies:
        copy.wait()


def spread_weights(plan, scalars, *arrays):
    hbm = pl.BlockSpec(memory_space=pl.ANY)
    return pl.pallas_call(
        functools.partial(spread_kernel, plan),
        grid_spec=pltpu.PrefetchScalarGridSpec(
            num_scalar_prefetch=1, grid=(1,), in_specs=[hbm] * 3,
            out_specs=pl.BlockSpec(memory_space=pltpu.VMEM),
            scratch_shapes=[pltpu.SemaphoreType.DMA((5 + 2 * plan.spots,))],
        ),
        out_shape=jax.ShapeDtypeStruct((SECTIONS, plan.packed, plan.width), BF),
        compiler_params=pltpu.CompilerParams(vmem_limit_bytes=plan.grant(SMALL_VMEM)),
        cost_estimate=pl.CostEstimate(flops=0, bytes_accessed=16 * plan.packed * plan.width, transcendentals=0),
    )(scalars, *arrays)


def grads_kernel(plan, latent, sc, mine, other, dir_first, gain_first, dir_second, gain_second, latents, cell_shape,
                 first_out, first_gain, first_bias, second_out, second_gain, second_bias, cells):
    core, spot = sc[1], sc[2]
    width, share, room, piece = plan.width, plan.share, plan.room, plan.piece
    for source, side in ((mine, core), (other, 1 - core)):
        for j in range(plan.spots):
            p = side * plan.spots + jnp.bitwise_xor(spot, j)
            base = j * piece
            rows = pl.ds(pl.multiple_of(p * share, share), share)
            second_out[rows, :] = source[base : base + share, :].astype(F32)
            first_out[rows, :] = source[base + share : base + 2 * share, :].astype(F32)
            rows = pl.ds(pl.multiple_of(p * room, room), room)
            cells[rows, :] = source[base + 2 * share : base + piece, :].astype(F32)
    by_cell = cells[...]
    shaped = jnp.where(cell_shape[...] >= 0, by_cell, 0.0)
    first_bias[...] = jnp.sum(shaped, axis=0, keepdims=True)
    shape = lax.broadcasted_iota(jnp.int32, (plan.cells, plan.shapes), 1)
    onehot = jnp.where(cell_shape[...] == shape, 1.0, 0.0).astype(BF)
    by_shape = mm(onehot, latents[...]).astype(BF)
    first_out[width : width + latent, :] = mm(by_shape, shaped.astype(BF), TN)
    for j in range(plan.coords):
        spot_row = plan.special(j)
        first_out[width + latent + j : width + latent + j + 1, :] = cells[spot_row : spot_row + 1, :]
    spot_row = plan.special(plan.coords)
    second_bias[...] = cells[spot_row : spot_row + 1, :]
    for direction, gain, out, gain_out in ((dir_first, gain_first, first_out, first_gain),
                                           (dir_second, gain_second, second_out, second_gain)):
        values = direction[...].astype(F32)
        summed = out[...]
        norm = jnp.sqrt(jnp.sum(values * values, axis=0, keepdims=True) + 1e-06)
        along = jnp.sum(values * summed, axis=0, keepdims=True)
        gain_out[...] = along / norm
        scale = gain[...].astype(F32) / norm
        out[...] = scale * summed - (scale * along / (norm * norm)) * values


def finish_grads(plan, scalars, mine, other, dir_first, gain_first, dir_second, gain_second, latents, cell_shape):
    width = plan.width
    vmem = pl.BlockSpec(memory_space=pltpu.VMEM)
    row = jax.ShapeDtypeStruct((1, width), F32)
    whole = lambda like: jax.ShapeDtypeStruct(like.shape, F32)
    return pl.pallas_call(
        functools.partial(grads_kernel, plan, latents.shape[1]),
        grid_spec=pltpu.PrefetchScalarGridSpec(
            num_scalar_prefetch=1, grid=(1,), in_specs=[vmem] * 8, out_specs=[vmem] * 6,
            scratch_shapes=[pltpu.VMEM((plan.cells, width), F32)],
        ),
        out_shape=[whole(dir_first), row, row, whole(dir_second), row, row],
        compiler_params=pltpu.CompilerParams(vmem_limit_bytes=plan.grant(SMALL_VMEM)),
        cost_estimate=pl.CostEstimate(flops=2 * plan.cells * width * latents.shape[1],
                                      bytes_accessed=8 * plan.packed * width, transcendentals=0),
    )(scalars, mine, other, dir_first, gain_first, dir_second, gain_second, latents, cell_shape)


def swap_section(block, distance):
    route = [(i, i ^ distance) for i in range(lax.axis_size("section"))]
    return lax.ppermute(block, "section", route)


def swap_dp(block, distance):
    route = [(i, i ^ distance) for i in range(lax.axis_size("dp"))]
    return lax.ppermute(block, "dp", route)


def cut(array, first, count):
    return lax.dynamic_slice_in_dim(array, first, count, 0)


def reduce_pieces(plan, chip, spot):
    piece = plan.piece
    total = cut(chip, spot * piece, piece).astype(F32)
    for distance in range(plan.spots - 1, 0, -1):
        away = jnp.bitwise_xor(spot, distance)
        total = total + swap_dp(cut(chip, away * piece, piece), 2 * distance).astype(F32)
    return total.astype(BF)


def gather_chips(plan, piece):
    got = [swap_dp(piece, 2 * distance) for distance in range(plan.spots - 1, 0, -1)]
    return [piece] + got[::-1]


def shards(
    inputs, cotangent, latent_codes, positions, shape_ids,
    direction_first, gain_first, bias_first, direction_second, gain_second, bias_second,
):
    section = lax.axis_index("section")
    dp_rank = lax.axis_index("dp")
    core, spot = dp_rank % 2, dp_rank // 2
    total, width = inputs.shape
    shapes, latent = latent_codes.shape
    coords = positions.shape[0]
    plan = Plan(width, coords, shapes, lax.axis_size("dp"))
    cell_shape = jnp.asarray(plan.cell_shape)
    place = jnp.stack([section, core, spot]).astype(jnp.int32)

    packed, skip, sending, far = pack_weights(
        plan, latent_codes, cell_shape,
        direction_first[0], gain_first, bias_first, direction_second[0], gain_second, bias_second,
    )
    far = swap_section(far, 3)
    sending, far = lax.optimization_barrier((sending, far))
    x_mine = swap_section(sending, 1)
    y_mine = swap_section(sending, 2)
    far_mine = gather_chips(plan, far)
    mine = join(plan, [x_mine, y_mine, *far_mine])
    weights = spread_weights(plan, place, packed, mine, swap_dp(mine, 1))

    blocks = total // ROWS
    ids = shape_ids.reshape(blocks, 1, ROWS)
    places = positions.reshape(coords, blocks, ROWS).transpose(1, 0, 2)
    same = (inputs, cotangent, ids, places, cell_shape, weights)
    given, parts, into, starts = [], [], [], []
    done = 0
    for steps in CALLS:
        *into, give_x, give_y, after_first, mine, theirs = run_blocks(
            plan, done, place, *same, into, (steps,), []
        )
        given.append((swap_section(give_x, 1), swap_section(give_y, 2), after_first))
        parts.append((mine, theirs))
        starts.append(done)
        done += steps
    for calls in HELPED_CALLS:
        sources = [source for call in calls for source in given[call]]
        counts = tuple(CALLS[call] for call in calls)
        *into, mine, theirs = run_blocks(plan, starts[calls[0]], place, *same, into, counts, sources)
        parts.append((mine, theirs))
    act, ig = into

    mine, theirs = (sum(part.astype(F32) for part in side) for side in zip(*parts))
    chip = (mine + swap_dp(theirs.astype(BF), 1).astype(F32)).astype(BF)
    piece = reduce_pieces(plan, chip, spot)
    pieces = gather_chips(plan, piece)
    ready, pieces[1] = lax.optimization_barrier((piece, pieces[1]))
    owned = mm(ready[2 * plan.share : 2 * plan.share + plan.owned], skip, NT)
    code = cut(owned, section * plan.per, plan.per)
    for distance in range(1, SECTIONS):
        away = jnp.bitwise_xor(section, distance)
        code = code + swap_section(cut(owned, away * plan.per, plan.per), distance)
    mine = join(plan, pieces)
    mine, code = lax.optimization_barrier((mine, code))
    other = swap_dp(mine, 1)
    first, first_gain, first_bias, second, second_gain, second_bias = finish_grads(
        plan, place, mine, other, direction_first[0], gain_first, direction_second[0], gain_second,
        latent_codes, cell_shape,
    )
    return (
        act[None], ig[None], code, first[None], first_gain, first_bias, second[None], second_gain, second_bias,
    )


def solution(mesh):
    in_specs = (
        P("dp", None), P("dp", None), P(), P(None, "dp"), P("dp"),
        P("section", None, None), P("section", None), P("section", None),
        P("section", None, None), P("section", None), P("section", None),
    )
    out_specs = (
        P("section", "dp", None), P("section", "dp", None), P(("section", "dp"), None),
        P("section", None, None), P("section", None), P("section", None),
        P("section", None, None), P("section", None), P("section", None),
    )
    return jax.shard_map(shards, mesh=mesh, in_specs=in_specs, out_specs=out_specs, check_vma=False)
```

profile of v0, /device:TPU:0, one launch (start us, length us, event | category | flops | bytes accessed | tf_op | source)
XLA Modules:
  0.0 175.1 jit_solution(14816238468695751572)
XLA Ops:
  0.6 3.4 %shard_map.187 = (bf16[1152,512]{1,0:T(8,128)(2,1)}, bf16[256,512]{1,0:T(8,128)(2,1)}, bf16[576,512]{1,0:T(8,128)(2,1)}, bf16[144,512]{1,0:T(8,128)(2,1)}) custom-call(bf16[771,512]{1,0:T(8,128)(2,1)} %bitcast.13, bf16[1,512]{1,0:T(2,128)(2,1)} %gain_first.1, bf16[1,512]{1,0:T(2,128)(2,1)} %refs_2_.1, bf16[512,512]{1,0:T(8,128)(2,1)} %bitcast.15, ...), custom_call_target="tpu_custom_call" | custom-call | flops 33554432 | bytes 2359296 | tf_op jit(solution)/shard_map/pallas_call | solution.py:438
  4.0 4.0 %collective-permute-start = (bf16[144,512]{1,0:T(8,128)(2,1)}, bf16[144,512]{1,0:T(8,128)(2,1)S(1)}, u32[]{:S(2)}, u32[]{:S(2)}) collective-permute-start(bf16[144,512]{1,0:T(8,128)(2,1)} %get-tuple-element.49), channel_id=1, source_target_pairs={{0,24},{8,16},{16,8},{24,0},{1,25},{9,17},{17,9},{25,1},{2,26},{10... | collective-permute-start | bytes 442376 | tf_op jit(solution)/shard_map/ppermute | solution.py:568
  8.0 4.1 %collective-permute-done.refs_2_ = bf16[144,512]{1,0:T(8,128)(2,1)S(1)} collective-permute-done((bf16[144,512]{1,0:T(8,128)(2,1)}, bf16[144,512]{1,0:T(8,128)(2,1)S(1)}, u32[]{:S(2)}, u32[]{:S(2)}) %collective-permute-start) | collective-permute-done | bytes 147488 | tf_op jit(solution)/shard_map/ppermute | solution.py:568
  16.8 2.6 %collective-permute-start.4 = (bf16[144,512]{1,0:T(8,128)(2,1)S(1)}, bf16[144,512]{1,0:T(8,128)(2,1)S(1)}, u32[]{:S(2)}, u32[]{:S(2)}) collective-permute-start(bf16[144,512]{1,0:T(8,128)(2,1)S(1)} %collective-permute-done.refs_2_), channel_id=1, source_target_pairs={{0,4},{1,5},{2,6},{3,7},{4,0},{5,1},{6,2},{7,3},{8,12},{9,13},{10,... | collective-permute-start | bytes 442376 | tf_op jit(solution)/shard_map/ppermute | solution.py:573
  19.6 2.0 %collective-permute-done.3.refs_3_ = bf16[144,512]{1,0:T(8,128)(2,1)S(1)} collective-permute-done((bf16[144,512]{1,0:T(8,128)(2,1)S(1)}, bf16[144,512]{1,0:T(8,128)(2,1)S(1)}, u32[]{:S(2)}, u32[]{:S(2)}) %collective-permute-start.3) | collective-permute-done | bytes 147488 | tf_op jit(solution)/shard_map/ppermute | solution.py:573
  21.7 7.8 %collective-permute-done.4.refs_4_ = bf16[144,512]{1,0:T(8,128)(2,1)S(1)} collective-permute-done((bf16[144,512]{1,0:T(8,128)(2,1)S(1)}, bf16[144,512]{1,0:T(8,128)(2,1)S(1)}, u32[]{:S(2)}, u32[]{:S(2)}) %collective-permute-start.4) | collective-permute-done | bytes 147488 | tf_op jit(solution)/shard_map/ppermute | solution.py:573
  32.2 2.2 %collective-permute-done.6.other = bf16[1728,512]{1,0:T(8,128)(2,1)S(1)} collective-permute-done((bf16[1728,512]{1,0:T(8,128)(2,1)S(1)}, bf16[1728,512]{1,0:T(8,128)(2,1)S(1)}, u32[]{:S(2)}, u32[]{:S(2)}) %collective-permute-start.6) | collective-permute-done | bytes 1769504 | tf_op jit(solution)/shard_map/ppermute | solution.py:573
  35.6 2.9 %shard_map.189.weights = bf16[4,1152,512]{2,1,0:T(8,128)(2,1)S(1)} custom-call(s32[3]{0:T(128)S(1)} %pad_add_fusion.sc, bf16[1152,512]{1,0:T(8,128)(2,1)S(1)} %copy-done.3, bf16[1728,512]{1,0:T(8,128)(2,1)S(1)} %shard_map.188.mine, bf16[1728,512]{1,0:T(8,128)(2,1)S(1)} %collective-permute-done.6.other), custom_call_target="tpu_custom_call" | custom-call | bytes 9437184 | tf_op jit(solution)/shard_map/pallas_call | solution.py:499
  38.9 33.9 %shard_map.190 = (bf16[7680,512]{1,0:T(8,128)(2,1)}, bf16[7680,512]{1,0:T(8,128)(2,1)}, bf16[1152,512]{1,0:T(8,128)(2,1)S(1)}, bf16[1152,512]{1,0:T(8,128)(2,1)S...) custom-call(s32[3]{0:T(128)S(1)} %pad_add_fusion.sc, ...), custom_call_target="tpu_custom_call" | custom-call | flops 25367150592 | bytes 14155776 | tf_op jit(solution)/shard_map/pallas_call | solution.py:382
  73.1 23.8 %shard_map.191 = (bf16[7680,512]{1,0:T(8,128)(2,1)}, bf16[7680,512]{1,0:T(8,128)(2,1)}, bf16[768,512]{1,0:T(8,128)(2,1)S(1)}, bf16[768,512]{1,0:T(8,128)(2,1)S(1...) custom-call(s32[3]{0:T(128)S(1)} %pad_add_fusion.sc, ...), custom_call_target="tpu_custom_call", output_to_operand_aliasing={{0}: (10, {}), {1}: (11, {})} | custom-call | flops 16911433728 | bytes 9437184 | tf_op jit(solution)/shard_map/pallas_call | solution.py:382
  98.5 3.1 %collective-permute-done.10.refs_1_ = bf16[1152,512]{1,0:T(8,128)(2,1)S(1)} collective-permute-done((bf16[1152,512]{1,0:T(8,128)(2,1)S(1)}, bf16[1152,512]{1,0:T(8,128)(2,1)S(1)}, u32[]{:S(2)}, u32[]{:S(2)}) %collective-permute-start.10) | collective-permute-done | bytes 1179680 | tf_op jit(solution)/shard_map/ppermute | solution.py:568
  102.0 14.0 %shard_map.192 = (bf16[7680,512]{1,0:T(8,128)(2,1)}, bf16[7680,512]{1,0:T(8,128)(2,1)}, bf16[576,512]{1,0:T(8,128)(2,1)S(1)}, bf16[576,512]{1,0:T(8,128)(2,1)S(1)}) custom-call(s32[3]{0:T(128)S(1)} %pad_add_fusion.sc, bf16[7680,512]{1,0:T(8,128)(2,1)S(1)} %copy-done, bf16[7680,512]{1,0:T(8,128)(2,1)} %g_in.7, ...), custom_call_target="tpu_custom_call", output_to_operand_aliasing={{0}: (10, {}), {1}: (11, {})} | custom-call | flops 9663676416 | bytes 14155776 | tf_op jit(solution)/shard_map/pallas_call | solution.py:382
  117.7 10.2 %shard_map.193 = (bf16[7680,512]{1,0:T(8,128)(2,1)}, bf16[7680,512]{1,0:T(8,128)(2,1)}, bf16[576,512]{1,0:T(8,128)(2,1)S(1)}, bf16[576,512]{1,0:T(8,128)(2,1)S(1)}) custom-call(s32[3]{0:T(128)S(1)} %pad_add_fusion.sc, bf16[7680,512]{1,0:T(8,128)(2,1)S(1)} %copy-done, bf16[7680,512]{1,0:T(8,128)(2,1)} %g_in.7, ...), custom_call_target="tpu_custom_call", output_to_operand_aliasing={{0}: (10, {}), {1}: (11, {})} | custom-call | flops 6442450944 | bytes 9437184 | tf_op jit(solution)/shard_map/pallas_call | solution.py:382
  128.3 2.0 %collective-permute-done.11 = bf16[576,512]{1,0:T(8,128)(2,1)S(1)} collective-permute-done((bf16[576,512]{1,0:T(8,128)(2,1)S(1)}, bf16[576,512]{1,0:T(8,128)(2,1)S(1)}, u32[]{:S(2)}, u32[]{:S(2)}) %collective-permute-start.11) | collective-permute-done | bytes 589856 | tf_op jit(solution)/shard_map/ppermute | solution.py:573
  130.8 3.0 %collective-permute-start.12 = (bf16[144,512]{1,0:T(8,128)(2,1)S(1)}, bf16[144,512]{1,0:T(8,128)(2,1)S(1)}, u32[]{:S(2)}, u32[]{:S(2)}) collective-permute-start(bf16[144,512]{1,0:T(8,128)(2,1)S(1)} %get-tuple-element.94), channel_id=1, source_target_pairs={{0,6},{1,7},{2,4},{3,5},{4,2},{5,3},{6,0},{7,1},{8,14},{9,15},{10,... | collective-permute-start | bytes 442376 | tf_op jit(solution)/shard_map/ppermute | solution.py:573
  135.3 4.2 %collective-permute-done.12 = bf16[144,512]{1,0:T(8,128)(2,1)S(1)} collective-permute-done((bf16[144,512]{1,0:T(8,128)(2,1)S(1)}, bf16[144,512]{1,0:T(8,128)(2,1)S(1)}, u32[]{:S(2)}, u32[]{:S(2)}) %collective-permute-start.12) | collective-permute-done | bytes 147488 | tf_op jit(solution)/shard_map/ppermute | solution.py:573
  139.5 8.3 %collective-permute-done.13 = bf16[144,512]{1,0:T(8,128)(2,1)S(1)} collective-permute-done((bf16[144,512]{1,0:T(8,128)(2,1)S(1)}, bf16[144,512]{1,0:T(8,128)(2,1)S(1)}, u32[]{:S(2)}, u32[]{:S(2)}) %collective-permute-start.13) | collective-permute-done | bytes 147488 | tf_op jit(solution)/shard_map/ppermute | solution.py:573
  148.0 3.0 %collective-permute-start.16 = (bf16[144,512]{1,0:T(8,128)(2,1)S(1)}, bf16[144,512]{1,0:T(8,128)(2,1)S(1)}, u32[]{:S(2)}, u32[]{:S(2)}) collective-permute-start(bf16[144,512]{1,0:T(8,128)(2,1)S(1)} %add_convert_fusion.2.refs_0_), channel_id=1, source_target_pairs={{0,4},{1,5},{2,6},{3,7},{4,0},{5,1},{6,2},{7,3},{8,12},{9,13},{10,... | collective-permute-start | bytes 442376 | tf_op jit(solution)/shard_map/ppermute | solution.py:573
  152.4 3.4 %collective-permute-done.15.refs_1_ = bf16[144,512]{1,0:T(8,128)(2,1)S(1)} collective-permute-done((bf16[144,512]{1,0:T(8,128)(2,1)S(1)}, bf16[144,512]{1,0:T(8,128)(2,1)S(1)}, u32[]{:S(2)}, u32[]{:S(2)}) %collective-permute-start.15) | collective-permute-done | bytes 147488 | tf_op jit(solution)/shard_map/ppermute | solution.py:573
  156.0 4.3 %collective-permute-start.18 = (f32[2,256]{1,0:T(2,128)S(1)}, f32[2,256]{1,0:T(2,128)S(1)}, u32[]{:S(2)}, u32[]{:S(2)}) collective-permute-start(f32[2,256]{1,0:T(2,128)S(1)} %get-tuple-element.97), channel_id=1, source_target_pairs={{0,8},{8,0},{16,24},{24,16},{1,9},{9,1},{17,25},{25,17},{2,10},{10... | collective-permute-start | bytes 6152 | tf_op jit(solution)/shard_map/ppermute | solution.py:568
  164.7 2.0 %collective-permute-done.20 = f32[2,256]{1,0:T(2,128)S(1)} collective-permute-done((f32[2,256]{1,0:T(2,128)S(1)}, f32[2,256]{1,0:T(2,128)S(1)}, u32[]{:S(2)}, u32[]{:S(2)}) %collective-permute-start.20) | collective-permute-done | bytes 2080 | tf_op jit(solution)/shard_map/ppermute | solution.py:568
  167.3 2.0 %collective-permute-done.21.other = bf16[576,512]{1,0:T(8,128)(2,1)S(1)} collective-permute-done((bf16[576,512]{1,0:T(8,128)(2,1)S(1)}, bf16[576,512]{1,0:T(8,128)(2,1)S(1)}, u32[]{:S(2)}, u32[]{:S(2)}) %collective-permute-start.21) | collective-permute-done | bytes 589856 | tf_op jit(solution)/shard_map/ppermute | solution.py:573
  169.3 3.0 %shard_map.195 = (f32[771,512]{1,0:T(8,128)S(1)}, f32[1,512]{1,0:T(1,128)}, f32[1,512]{1,0:T(1,128)}, f32[512,512]{1,0:T(8,128)}, f32[1,512]{1,0:T(1,128)}, /*index=5*/f32[1,512]{1,0:T(1,128)}) custom-call(s32[3]{0:T(128)S(1)} %pad_add_fusion.sc, bf16[576,512]{1,0:T(8,128)(2,1)S(1)} %shard_map.194.mine, bf16[576,512]{1,0:T(8,128)(2,1)S(1)} %collective-permute-done.21.other, ...), custom_call_target="tpu_custom_call" | custom-call | flops 33554432 | bytes 4718592 | tf_op jit(solution)/shard_map/pallas_call | solution.py:553
  172.3 2.8 %copy.27 = f32[1,771,512]{2,0,1:T(1,128)} copy(f32[1,771,512]{2,1,0:T(8,128)S(1)} %bitcast.17) | data formatting | bytes 3158016
  (63 shorter events, 22.3 us)
Async XLA Ops:
  4.0 8.0 %collective-permute-start = (bf16[144,512]{1,0:T(8,128)(2,1)}, bf16[144,512]{1,0:T(8,128)(2,1)S(1)}, u32[]{:S(2)}, u32[]{:S(2)}) collective-permute-start(bf16[144,512]{1,0:T(8,128)(2,1)} %get-tuple-element.49), channel_id=1, source_target_pairs={{0,24},{8,16},{16,8},{24,0},{1,25},{9,17},{17,9},{25,1},{2,26},{10... | collective-permute-start | bytes 442376 | tf_op jit(solution)/shard_map/ppermute | solution.py:568
  12.0 17.5 %collective-permute-start.1 = (bf16[576,512]{1,0:T(8,128)(2,1)}, bf16[576,512]{1,0:T(8,128)(2,1)S(1)}, u32[]{:S(2)}, u32[]{:S(2)}) collective-permute-start(bf16[576,512]{1,0:T(8,128)(2,1)} %get-tuple-element.50), channel_id=1, source_target_pairs={{0,8},{8,0},{16,24},{24,16},{1,9},{9,1},{17,25},{25,17},{2,10},{10... | collective-permute-start | bytes 1769480 | tf_op jit(solution)/shard_map/ppermute | solution.py:568
  13.7 15.8 %collective-permute-start.2 = (bf16[576,512]{1,0:T(8,128)(2,1)}, bf16[576,512]{1,0:T(8,128)(2,1)S(1)}, u32[]{:S(2)}, u32[]{:S(2)}) collective-permute-start(bf16[576,512]{1,0:T(8,128)(2,1)} %get-tuple-element.50), channel_id=1, source_target_pairs={{0,16},{8,24},{16,0},{24,8},{1,17},{9,25},{17,1},{25,9},{2,18},{10... | collective-permute-start | bytes 1769480 | tf_op jit(solution)/shard_map/ppermute | solution.py:568
  15.2 6.4 %collective-permute-start.3 = (bf16[144,512]{1,0:T(8,128)(2,1)S(1)}, bf16[144,512]{1,0:T(8,128)(2,1)S(1)}, u32[]{:S(2)}, u32[]{:S(2)}) collective-permute-start(bf16[144,512]{1,0:T(8,128)(2,1)S(1)} %collective-permute-done.refs_2_), channel_id=1, source_target_pairs={{0,2},{1,3},{2,0},{3,1},{4,6},{5,7},{6,4},{7,5},{8,10},{9,11},{10,... | collective-permute-start | bytes 442376 | tf_op jit(solution)/shard_map/ppermute | solution.py:573
  16.8 12.7 %collective-permute-start.4 = (bf16[144,512]{1,0:T(8,128)(2,1)S(1)}, bf16[144,512]{1,0:T(8,128)(2,1)S(1)}, u32[]{:S(2)}, u32[]{:S(2)}) collective-permute-start(bf16[144,512]{1,0:T(8,128)(2,1)S(1)} %collective-permute-done.refs_2_), channel_id=1, source_target_pairs={{0,4},{1,5},{2,6},{3,7},{4,0},{5,1},{6,2},{7,3},{8,12},{9,13},{10,... | collective-permute-start | bytes 442376 | tf_op jit(solution)/shard_map/ppermute | solution.py:573
  19.4 10.1 %collective-permute-start.5 = (bf16[144,512]{1,0:T(8,128)(2,1)S(1)}, bf16[144,512]{1,0:T(8,128)(2,1)S(1)}, u32[]{:S(2)}, u32[]{:S(2)}) collective-permute-start(bf16[144,512]{1,0:T(8,128)(2,1)S(1)} %collective-permute-done.refs_2_), channel_id=1, source_target_pairs={{0,6},{1,7},{2,4},{3,5},{4,2},{5,3},{6,0},{7,1},{8,14},{9,15},{10,... | collective-permute-start | bytes 442376 | tf_op jit(solution)/shard_map/ppermute | solution.py:573
  30.6 3.8 %collective-permute-start.6 = (bf16[1728,512]{1,0:T(8,128)(2,1)S(1)}, bf16[1728,512]{1,0:T(8,128)(2,1)S(1)}, u32[]{:S(2)}, u32[]{:S(2)}) collective-permute-start(bf16[1728,512]{1,0:T(8,128)(2,1)S(1)} %shard_map.188.mine), channel_id=1, source_target_pairs={{0,1},{1,0},{2,3},{3,2},{4,5},{5,4},{6,7},{7,6},{8,9},{9,8},{10,11... | collective-permute-start | bytes 5308424 | tf_op jit(solution)/shard_map/ppermute | solution.py:573
  72.7 28.8 %collective-permute-start.10 = (bf16[1152,512]{1,0:T(8,128)(2,1)S(1)}, bf16[1152,512]{1,0:T(8,128)(2,1)S(1)}, u32[]{:S(2)}, u32[]{:S(2)}) collective-permute-start(bf16[1152,512]{1,0:T(8,128)(2,1)S(1)} %get-tuple-element.58), channel_id=1, source_target_pairs={{0,16},{8,24},{16,0},{24,8},{1,17},{9,25},{17,1},{25,9},{2,18},{10... | collective-permute-start | bytes 3538952 | tf_op jit(solution)/shard_map/ppermute | solution.py:568
  73.1 28.9 %collective-permute-start.9 = (bf16[1152,512]{1,0:T(8,128)(2,1)S(1)}, bf16[1152,512]{1,0:T(8,128)(2,1)S(1)}, u32[]{:S(2)}, u32[]{:S(2)}) collective-permute-start(bf16[1152,512]{1,0:T(8,128)(2,1)S(1)} %get-tuple-element.57), channel_id=1, source_target_pairs={{0,8},{8,0},{16,24},{24,16},{1,9},{9,1},{17,25},{25,17},{2,10},{10... | collective-permute-start | bytes 3538952 | tf_op jit(solution)/shard_map/ppermute | solution.py:568
  96.9 20.8 %collective-permute-start.7 = (bf16[768,512]{1,0:T(8,128)(2,1)S(1)}, bf16[768,512]{1,0:T(8,128)(2,1)S(1)}, u32[]{:S(2)}, u32[]{:S(2)}) collective-permute-start(bf16[768,512]{1,0:T(8,128)(2,1)S(1)} %get-tuple-element.54), channel_id=1, source_target_pairs={{0,8},{8,0},{16,24},{24,16},{1,9},{9,1},{17,25},{25,17},{2,10},{10... | collective-permute-start | bytes 2359304 | tf_op jit(solution)/shard_map/ppermute | solution.py:568
  96.9 20.8 %collective-permute-start.8 = (bf16[768,512]{1,0:T(8,128)(2,1)S(1)}, bf16[768,512]{1,0:T(8,128)(2,1)S(1)}, u32[]{:S(2)}, u32[]{:S(2)}) collective-permute-start(bf16[768,512]{1,0:T(8,128)(2,1)S(1)} %get-tuple-element.55), channel_id=1, source_target_pairs={{0,16},{8,24},{16,0},{24,8},{1,17},{9,25},{17,1},{25,9},{2,18},{10... | collective-permute-start | bytes 2359304 | tf_op jit(solution)/shard_map/ppermute | solution.py:568
  128.2 2.1 %collective-permute-start.11 = (bf16[576,512]{1,0:T(8,128)(2,1)S(1)}, bf16[576,512]{1,0:T(8,128)(2,1)S(1)}, u32[]{:S(2)}, u32[]{:S(2)}) collective-permute-start(bf16[576,512]{1,0:T(8,128)(2,1)S(1)} %add_convert_fusion.1), channel_id=1, source_target_pairs={{0,1},{1,0},{2,3},{3,2},{4,5},{5,4},{6,7},{7,6},{8,9},{9,8},{10,11... | collective-permute-start | bytes 1769480 | tf_op jit(solution)/shard_map/ppermute | solution.py:573
  130.7 38.5 %copy-start.1 = (bf16[1,771,512]{2,1,0:T(8,128)(2,1)S(1)}, bf16[1,771,512]{2,1,0:T(8,128)(2,1)}, u32[]{:S(2)}) copy-start(bf16[1,771,512]{2,1,0:T(8,128)(2,1)} %param.17) | copy-start | bytes 2368516
  130.8 38.5 %copy-start.2 = (bf16[1,512,512]{2,1,0:T(8,128)(2,1)S(1)}, bf16[1,512,512]{2,1,0:T(8,128)(2,1)}, u32[]{:S(2)}) copy-start(bf16[1,512,512]{2,1,0:T(8,128)(2,1)} %param.20) | copy-start | bytes 1572868
  130.8 8.7 %collective-permute-start.12 = (bf16[144,512]{1,0:T(8,128)(2,1)S(1)}, bf16[144,512]{1,0:T(8,128)(2,1)S(1)}, u32[]{:S(2)}, u32[]{:S(2)}) collective-permute-start(bf16[144,512]{1,0:T(8,128)(2,1)S(1)} %get-tuple-element.94), channel_id=1, source_target_pairs={{0,6},{1,7},{2,4},{3,5},{4,2},{5,3},{6,0},{7,1},{8,14},{9,15},{10,... | collective-permute-start | bytes 442376 | tf_op jit(solution)/shard_map/ppermute | solution.py:573
  133.8 14.0 %collective-permute-start.13 = (bf16[144,512]{1,0:T(8,128)(2,1)S(1)}, bf16[144,512]{1,0:T(8,128)(2,1)S(1)}, u32[]{:S(2)}, u32[]{:S(2)}) collective-permute-start(bf16[144,512]{1,0:T(8,128)(2,1)S(1)} %get-tuple-element.96), channel_id=1, source_target_pairs={{0,4},{1,5},{2,6},{3,7},{4,0},{5,1},{6,2},{7,3},{8,12},{9,13},{10,... | collective-permute-start | bytes 442376 | tf_op jit(solution)/shard_map/ppermute | solution.py:573
  134.5 13.3 %collective-permute-start.14 = (bf16[144,512]{1,0:T(8,128)(2,1)S(1)}, bf16[144,512]{1,0:T(8,128)(2,1)S(1)}, u32[]{:S(2)}, u32[]{:S(2)}) collective-permute-start(bf16[144,512]{1,0:T(8,128)(2,1)S(1)} %get-tuple-element.95), channel_id=1, source_target_pairs={{0,2},{1,3},{2,0},{3,1},{4,6},{5,7},{6,4},{7,5},{8,10},{9,11},{10,... | collective-permute-start | bytes 442376 | tf_op jit(solution)/shard_map/ppermute | solution.py:573
  147.9 7.9 %collective-permute-start.15 = (bf16[144,512]{1,0:T(8,128)(2,1)S(1)}, bf16[144,512]{1,0:T(8,128)(2,1)S(1)}, u32[]{:S(2)}, u32[]{:S(2)}) collective-permute-start(bf16[144,512]{1,0:T(8,128)(2,1)S(1)} %add_convert_fusion.2.refs_0_), channel_id=1, source_target_pairs={{0,2},{1,3},{2,0},{3,1},{4,6},{5,7},{6,4},{7,5},{8,10},{9,11},{10,... | collective-permute-start | bytes 442376 | tf_op jit(solution)/shard_map/ppermute | solution.py:573
  148.0 15.6 %collective-permute-start.16 = (bf16[144,512]{1,0:T(8,128)(2,1)S(1)}, bf16[144,512]{1,0:T(8,128)(2,1)S(1)}, u32[]{:S(2)}, u32[]{:S(2)}) collective-permute-start(bf16[144,512]{1,0:T(8,128)(2,1)S(1)} %add_convert_fusion.2.refs_0_), channel_id=1, source_target_pairs={{0,4},{1,5},{2,6},{3,7},{4,0},{5,1},{6,2},{7,3},{8,12},{9,13},{10,... | collective-permute-start | bytes 442376 | tf_op jit(solution)/shard_map/ppermute | solution.py:573
  151.1 12.5 %collective-permute-start.17 = (bf16[144,512]{1,0:T(8,128)(2,1)S(1)}, bf16[144,512]{1,0:T(8,128)(2,1)S(1)}, u32[]{:S(2)}, u32[]{:S(2)}) collective-permute-start(bf16[144,512]{1,0:T(8,128)(2,1)S(1)} %add_convert_fusion.2.refs_0_), channel_id=1, source_target_pairs={{0,6},{1,7},{2,4},{3,5},{4,2},{5,3},{6,0},{7,1},{8,14},{9,15},{10,... | collective-permute-start | bytes 442376 | tf_op jit(solution)/shard_map/ppermute | solution.py:573
  156.0 8.7 %collective-permute-start.18 = (f32[2,256]{1,0:T(2,128)S(1)}, f32[2,256]{1,0:T(2,128)S(1)}, u32[]{:S(2)}, u32[]{:S(2)}) collective-permute-start(f32[2,256]{1,0:T(2,128)S(1)} %get-tuple-element.97), channel_id=1, source_target_pairs={{0,8},{8,0},{16,24},{24,16},{1,9},{9,1},{17,25},{25,17},{2,10},{10... | collective-permute-start | bytes 6152 | tf_op jit(solution)/shard_map/ppermute | solution.py:568
  160.3 4.4 %collective-permute-start.19 = (f32[2,256]{1,0:T(2,128)S(1)}, f32[2,256]{1,0:T(2,128)S(1)}, u32[]{:S(2)}, u32[]{:S(2)}) collective-permute-start(f32[2,256]{1,0:T(2,128)S(1)} %get-tuple-element.99), channel_id=1, source_target_pairs={{0,16},{8,24},{16,0},{24,8},{1,17},{9,25},{17,1},{25,9},{2,18},{10... | collective-permute-start | bytes 6152 | tf_op jit(solution)/shard_map/ppermute | solution.py:568
  162.2 4.5 %collective-permute-start.20 = (f32[2,256]{1,0:T(2,128)S(1)}, f32[2,256]{1,0:T(2,128)S(1)}, u32[]{:S(2)}, u32[]{:S(2)}) collective-permute-start(f32[2,256]{1,0:T(2,128)S(1)} %get-tuple-element.98), channel_id=1, source_target_pairs={{0,24},{8,16},{16,8},{24,0},{1,25},{9,17},{17,9},{25,1},{2,26},{10... | collective-permute-start | bytes 6152 | tf_op jit(solution)/shard_map/ppermute | solution.py:568
  167.3 2.0 %collective-permute-start.21 = (bf16[576,512]{1,0:T(8,128)(2,1)S(1)}, bf16[576,512]{1,0:T(8,128)(2,1)S(1)}, u32[]{:S(2)}, u32[]{:S(2)}) collective-permute-start(bf16[576,512]{1,0:T(8,128)(2,1)S(1)} %shard_map.194.mine), channel_id=1, source_target_pairs={{0,1},{1,0},{2,3},{3,2},{4,5},{5,4},{6,7},{7,6},{8,9},{9,8},{10,11... | collective-permute-start | bytes 1769480 | tf_op jit(solution)/shard_map/ppermute | solution.py:573
  (10 other events, 193.4 us)
where the time goes:
time: 176 us; the launch traced here: 175 us
  Pallas kernels  93.2 us (53%)
  waiting for transfers between devices  43.4 us (25%)
  starting transfers between devices  30.2 us (17%)
  local copies, waits for them, and re-layouts  5.84 us (3%)
    pallas_call x4, Pallas kernels, run_blocks(): pl.pallas_call(kernel, grid_spec=pltpu.PrefetchScalarGridSpec(num_scalar_...  81.8 us
    ppermute x12, waiting for transfers between devices, swap_dp(): return lax.ppermute(block, 'dp', route)  32 us
    ppermute x10, starting transfers between devices, swap_section(): return lax.ppermute(block, 'section', route)  16.7 us
    ppermute x12, starting transfers between devices, swap_dp(): return lax.ppermute(block, 'dp', route)  13.4 us
    ppermute x10, waiting for transfers between devices, swap_section(): return lax.ppermute(block, 'section', route)  11.4 us
    unnamed x25, local copies, waits for them, and re-layouts  4.37 us
  transfers between devices with their start and end apart: 22, of which 13 were waited for; matrix products, arithmetic and copies ran while one was open for 1% of the time, Pallas kernels for 22%

commit v1 on v0

--- a/solution.py
+++ b/solution.py
@@ -473,20 +473,19 @@
     )(*arrays)
 
 
-def spread_kernel(plan, sc, own, mine, other, weights, sems):
+def spread_kernel(plan, near, sc, *refs):
     section, core, spot = sc[0], sc[1], sc[2]
     half, piece = plan.half, plan.piece
-    away = 1 - core
-    copies = [(own, weights.at[section])]
+    first, block, weights, sems = refs
+    side = core if near else 1 - core
+    copies = [(first, weights.at[section])] if near else []
     for j in range(2):
         there = weights.at[jnp.bitwise_xor(section, j + 1)]
-        for block, side in ((mine, core), (other, away)):
-            copies.append((block.at[pl.ds(j * half, half)], there.at[pl.ds(side * half, half)]))
+        copies.append((block.at[pl.ds(j * half, half)], there.at[pl.ds(side * half, half)]))
     there = weights.at[jnp.bitwise_xor(section, 3)]
     for j in range(plan.spots):
         z = jnp.bitwise_xor(spot, j)
-        for block, side in ((mine, core), (other, away)):
-            copies.append((block.at[pl.ds(2 * half + j * piece, piece)], there.at[pl.ds(side * half + z * piece, piece)]))
+        copies.append((block.at[pl.ds(2 * half + j * piece, piece)], there.at[pl.ds(side * half + z * piece, piece)]))
     copies = [pltpu.make_async_copy(source, target, sems.at[j]) for j, (source, target) in enumerate(copies)]
     for copy in copies:
         copy.start()
@@ -494,23 +493,24 @@
         copy.wait()
 
 
-def spread_weights(plan, scalars, *arrays):
+def spread_weights(plan, near, scalars, first, block):
     hbm = pl.BlockSpec(memory_space=pl.ANY)
+    vmem = pl.BlockSpec(memory_space=pltpu.VMEM)
     return pl.pallas_call(
-        functools.partial(spread_kernel, plan),
+        functools.partial(spread_kernel, plan, near),
         grid_spec=pltpu.PrefetchScalarGridSpec(
-            num_scalar_prefetch=1, grid=(1,), in_specs=[hbm] * 3,
-            out_specs=pl.BlockSpec(memory_space=pltpu.VMEM),
-            scratch_shapes=[pltpu.SemaphoreType.DMA((5 + 2 * plan.spots,))],
+            num_scalar_prefetch=1, grid=(1,), in_specs=[hbm if near else vmem, hbm], out_specs=vmem,
+            scratch_shapes=[pltpu.SemaphoreType.DMA((3 + plan.spots,))],
         ),
         out_shape=jax.ShapeDtypeStruct((SECTIONS, plan.packed, plan.width), BF),
+        input_output_aliases={} if near else {1: 0},
         compiler_params=pltpu.CompilerParams(vmem_limit_bytes=plan.grant(SMALL_VMEM)),
-        cost_estimate=pl.CostEstimate(flops=0, bytes_accessed=16 * plan.packed * plan.width, transcendentals=0),
-    )(scalars, *arrays)
+        cost_estimate=pl.CostEstimate(flops=0, bytes_accessed=8 * plan.packed * plan.width, transcendentals=0),
+    )(scalars, first, block)
 
 
 def grads_kernel(plan, latent, sc, mine, other, dir_first, gain_first, dir_second, gain_second, latents, cell_shape,
-                 first_out, first_gain, first_bias, second_out, second_gain, second_bias, cells):
+                 first_rows, first_gain, first_bias, second_out, second_gain, second_bias, cells, first_out):
     core, spot = sc[1], sc[2]
     width, share, room, piece = plan.width, plan.share, plan.room, plan.piece
     for source, side in ((mine, core), (other, 1 - core)):
@@ -542,7 +542,12 @@
         along = jnp.sum(values * summed, axis=0, keepdims=True)
         gain_out[...] = along / norm
         scale = gain[...].astype(F32) / norm
-        out[...] = scale * summed - (scale * along / (norm * norm)) * values
+        result = scale * summed - (scale * along / (norm * norm)) * values
+        if out is first_out:
+            for j in range(first_rows.shape[1]):
+                first_rows[:, j, :] = result[:, j * 128 : (j + 1) * 128]
+        else:
+            out[...] = result
 
 
 def finish_grads(plan, scalars, mine, other, dir_first, gain_first, dir_second, gain_second, latents, cell_shape):
@@ -554,9 +559,9 @@
         functools.partial(grads_kernel, plan, latents.shape[1]),
         grid_spec=pltpu.PrefetchScalarGridSpec(
             num_scalar_prefetch=1, grid=(1,), in_specs=[vmem] * 8, out_specs=[vmem] * 6,
-            scratch_shapes=[pltpu.VMEM((plan.cells, width), F32)],
+            scratch_shapes=[pltpu.VMEM((plan.cells, width), F32), pltpu.VMEM(dir_first.shape, F32)],
         ),
-        out_shape=[whole(dir_first), row, row, whole(dir_second), row, row],
+        out_shape=[jax.ShapeDtypeStruct((dir_first.shape[0], width // 128, 128), F32), row, row, whole(dir_second), row, row],
         compiler_params=pltpu.CompilerParams(vmem_limit_bytes=plan.grant(SMALL_VMEM)),
         cost_estimate=pl.CostEstimate(flops=2 * plan.cells * width * latents.shape[1],
                                       bytes_accessed=8 * plan.packed * width, transcendentals=0),
@@ -609,17 +614,19 @@
         plan, latent_codes, cell_shape,
         direction_first[0], gain_first, bias_first, direction_second[0], gain_second, bias_second,
     )
+    blocks = total // ROWS
+    ids = shape_ids.reshape(blocks, 1, ROWS)
+    places = positions.reshape(coords, blocks, ROWS).transpose(1, 0, 2)
     far = swap_section(far, 3)
-    sending, far = lax.optimization_barrier((sending, far))
+    sending, far, ids, places, place = lax.optimization_barrier((sending, far, ids, places, place))
     x_mine = swap_section(sending, 1)
     y_mine = swap_section(sending, 2)
     far_mine = gather_chips(plan, far)
     mine = join(plan, [x_mine, y_mine, *far_mine])
-    weights = spread_weights(plan, place, packed, mine, swap_dp(mine, 1))
-
-    blocks = total // ROWS
-    ids = shape_ids.reshape(blocks, 1, ROWS)
-    places = positions.reshape(coords, blocks, ROWS).transpose(1, 0, 2)
+    other = swap_dp(mine, 1)
+    weights = spread_weights(plan, True, place, packed, mine)
+    weights = spread_weights(plan, False, place, weights, other)
+
     same = (inputs, cotangent, ids, places, cell_shape, weights)
     given, parts, into, starts = [], [], [], []
     done = 0
@@ -656,7 +663,7 @@
         latent_codes, cell_shape,
     )
     return (
-        act[None], ig[None], code, first[None], first_gain, first_bias, second[None], second_gain, second_bias,
+        act[None], ig[None], code, first.reshape(direction_first.shape), first_gain, first_bias, second[None], second_gain, second_bias,
     )
 
 

time: 176 us -> 172 us (0.977)
  local copies, waits for them, and re-layouts: 5.84 us -> 0.68 us
    unnamed x25 -> x26, local copies, waits for them, and re-layouts: 4.37 us -> 0.57 us
    pallas_call x4, Pallas kernels: 81.8 us -> 79.8 us  [run_blocks(): pl.pallas_call(kernel, grid_spec=pltpu.PrefetchScalarGridSpec(num_scalar_...]
  transfers between devices with their start and end apart: 22 -> 22, of which waited for: 13 -> 13; matrix products, arithmetic and copies ran while one was open for 1% -> 0% of each run, Pallas kernels for 22% -> 23%
where the time goes in v1:
time: 172 us; the launch traced here: 171 us
  Pallas kernels  92.8 us (54%)
  waiting for transfers between devices  43.7 us (25%)
  starting transfers between devices  29.8 us (17%)
  other arithmetic  2.52 us (1%)
    pallas_call x4, Pallas kernels, run_blocks(): pl.pallas_call(kernel, grid_spec=pltpu.PrefetchScalarGridSpec(num_scalar_...  79.8 us
    ppermute x12, waiting for transfers between devices, swap_dp(): return lax.ppermute(block, 'dp', route)  31.6 us
    ppermute x10, starting transfers between devices, swap_section(): return lax.ppermute(block, 'section', route)  16.4 us
    ppermute x12, starting transfers between devices, swap_dp(): return lax.ppermute(block, 'dp', route)  13.3 us
    ppermute x10, waiting for transfers between devices, swap_section(): return lax.ppermute(block, 'section', route)  12.1 us
    pallas_call x1, Pallas kernels, finish_grads(): pl.pallas_call(functools.partial(grads_kernel, plan, latents.shape[1]), g...  3.99 us
    pallas_call x2, Pallas kernels, spread_weights(): pl.pallas_call(functools.partial(spread_kernel, plan, near), grid_spec=pl...  3.49 us
  transfers between devices with their start and end apart: 22, of which 13 were waited for; matrix products, arithmetic and copies ran while one was open for 0% of the time, Pallas kernels for 23%

profile of v1, /device:TPU:0, one launch (start us, length us, event | category | flops | bytes accessed | tf_op | source)
XLA Modules:
  0.0 170.6 jit_solution(15674532654144368090)
XLA Ops:
  0.7 3.4 %shard_map.187 = (bf16[1152,512]{1,0:T(8,128)(2,1)}, bf16[256,512]{1,0:T(8,128)(2,1)}, bf16[576,512]{1,0:T(8,128)(2,1)}, bf16[144,512]{1,0:T(8,128)(2,1)}) custom-call(bf16[771,512]{1,0:T(8,128)(2,1)} %bitcast.15, bf16[1,512]{1,0:T(2,128)(2,1)} %gain_first.1, bf16[1,512]{1,0:T(2,128)(2,1)} %refs_2_.1, bf16[512,512]{1,0:T(8,128)(2,1)} %bitcast.17, ...), custom_call_target="tpu_custom_call" | custom-call | flops 33554432 | bytes 2359296 | tf_op jit(solution)/shard_map/pallas_call | solution.py:438
  4.0 4.0 %collective-permute-start = (bf16[144,512]{1,0:T(8,128)(2,1)}, bf16[144,512]{1,0:T(8,128)(2,1)S(1)}, u32[]{:S(2)}, u32[]{:S(2)}) collective-permute-start(bf16[144,512]{1,0:T(8,128)(2,1)} %get-tuple-element.51), channel_id=1, source_target_pairs={{0,24},{8,16},{16,8},{24,0},{1,25},{9,17},{17,9},{25,1},{2,26},{10... | collective-permute-start | bytes 442376 | tf_op jit(solution)/shard_map/ppermute | solution.py:573
  8.1 3.9 %collective-permute-done.refs_2_ = bf16[144,512]{1,0:T(8,128)(2,1)S(1)} collective-permute-done((bf16[144,512]{1,0:T(8,128)(2,1)}, bf16[144,512]{1,0:T(8,128)(2,1)S(1)}, u32[]{:S(2)}, u32[]{:S(2)}) %collective-permute-start) | collective-permute-done | bytes 147488 | tf_op jit(solution)/shard_map/ppermute | solution.py:573
  16.8 2.6 %collective-permute-start.4 = (bf16[144,512]{1,0:T(8,128)(2,1)S(1)}, bf16[144,512]{1,0:T(8,128)(2,1)S(1)}, u32[]{:S(2)}, u32[]{:S(2)}) collective-permute-start(bf16[144,512]{1,0:T(8,128)(2,1)S(1)} %collective-permute-done.refs_2_), channel_id=1, source_target_pairs={{0,4},{1,5},{2,6},{3,7},{4,0},{5,1},{6,2},{7,3},{8,12},{9,13},{10,... | collective-permute-start | bytes 442376 | tf_op jit(solution)/shard_map/ppermute | solution.py:578
  19.7 2.0 %collective-permute-done.3.refs_3_ = bf16[144,512]{1,0:T(8,128)(2,1)S(1)} collective-permute-done((bf16[144,512]{1,0:T(8,128)(2,1)S(1)}, bf16[144,512]{1,0:T(8,128)(2,1)S(1)}, u32[]{:S(2)}, u32[]{:S(2)}) %collective-permute-start.3) | collective-permute-done | bytes 147488 | tf_op jit(solution)/shard_map/ppermute | solution.py:578
  21.7 7.8 %collective-permute-done.4.refs_4_ = bf16[144,512]{1,0:T(8,128)(2,1)S(1)} collective-permute-done((bf16[144,512]{1,0:T(8,128)(2,1)S(1)}, bf16[144,512]{1,0:T(8,128)(2,1)S(1)}, u32[]{:S(2)}, u32[]{:S(2)}) %collective-permute-start.4) | collective-permute-done | bytes 147488 | tf_op jit(solution)/shard_map/ppermute | solution.py:578
  30.7 1.9 %shard_map.189.refs_0_ = bf16[4,1152,512]{2,1,0:T(8,128)(2,1)S(1)} custom-call(s32[3]{0:T(128)S(1)} %pad_add_fusion.sc, bf16[1152,512]{1,0:T(8,128)(2,1)S(1)} %copy-done.2, bf16[1728,512]{1,0:T(8,128)(2,1)S(1)} %shard_map.188.refs_1_), custom_call_target="tpu_custom_call" | custom-call | bytes 4718592 | tf_op jit(solution)/shard_map/pallas_call | solution.py:499
  36.0 33.0 %shard_map.191 = (bf16[7680,512]{1,0:T(8,128)(2,1)}, bf16[7680,512]{1,0:T(8,128)(2,1)}, bf16[1152,512]{1,0:T(8,128)(2,1)S(1)}, bf16[1152,512]{1,0:T(8,128)(2,1)S...) custom-call(s32[3]{0:T(128)S(1)} %pad_add_fusion.sc, ...), custom_call_target="tpu_custom_call" | custom-call | flops 25367150592 | bytes 14155776 | tf_op jit(solution)/shard_map/pallas_call | solution.py:382
  69.4 23.2 %shard_map.192 = (bf16[7680,512]{1,0:T(8,128)(2,1)}, bf16[7680,512]{1,0:T(8,128)(2,1)}, bf16[768,512]{1,0:T(8,128)(2,1)S(1)}, bf16[768,512]{1,0:T(8,128)(2,1)S(1...) custom-call(s32[3]{0:T(128)S(1)} %pad_add_fusion.sc, ...), custom_call_target="tpu_custom_call", output_to_operand_aliasing={{0}: (10, {}), {1}: (11, {})} | custom-call | flops 16911433728 | bytes 9437184 | tf_op jit(solution)/shard_map/pallas_call | solution.py:382
  94.1 3.7 %collective-permute-done.10.refs_1_ = bf16[1152,512]{1,0:T(8,128)(2,1)S(1)} collective-permute-done((bf16[1152,512]{1,0:T(8,128)(2,1)S(1)}, bf16[1152,512]{1,0:T(8,128)(2,1)S(1)}, u32[]{:S(2)}, u32[]{:S(2)}) %collective-permute-start.10) | collective-permute-done | bytes 1179680 | tf_op jit(solution)/shard_map/ppermute | solution.py:573
  98.3 13.7 %shard_map.193 = (bf16[7680,512]{1,0:T(8,128)(2,1)}, bf16[7680,512]{1,0:T(8,128)(2,1)}, bf16[576,512]{1,0:T(8,128)(2,1)S(1)}, bf16[576,512]{1,0:T(8,128)(2,1)S(1)}) custom-call(s32[3]{0:T(128)S(1)} %pad_add_fusion.sc, bf16[7680,512]{1,0:T(8,128)(2,1)S(1)} %bitcast.14, bf16[7680,512]{1,0:T(8,128)(2,1)} %g_in.7, ...), custom_call_target="tpu_custom_call", output_to_operand_aliasing={{0}: (10, {}), {1}: (11, {})} | custom-call | flops 9663676416 | bytes 14155776 | tf_op jit(solution)/shard_map/pallas_call | solution.py:382
  112.0 2.0 %collective-permute-done.7.refs_0_ = bf16[768,512]{1,0:T(8,128)(2,1)S(1)} collective-permute-done((bf16[768,512]{1,0:T(8,128)(2,1)S(1)}, bf16[768,512]{1,0:T(8,128)(2,1)S(1)}, u32[]{:S(2)}, u32[]{:S(2)}) %collective-permute-start.7) | collective-permute-done | bytes 786464 | tf_op jit(solution)/shard_map/ppermute | solution.py:573
  114.0 10.0 %shard_map.194 = (bf16[7680,512]{1,0:T(8,128)(2,1)}, bf16[7680,512]{1,0:T(8,128)(2,1)}, bf16[576,512]{1,0:T(8,128)(2,1)S(1)}, bf16[576,512]{1,0:T(8,128)(2,1)S(1)}) custom-call(s32[3]{0:T(128)S(1)} %pad_add_fusion.sc, bf16[7680,512]{1,0:T(8,128)(2,1)S(1)} %bitcast.14, bf16[7680,512]{1,0:T(8,128)(2,1)} %g_in.7, ...), custom_call_target="tpu_custom_call", output_to_operand_aliasing={{0}: (10, {}), {1}: (11, {})} | custom-call | flops 6442450944 | bytes 9437184 | tf_op jit(solution)/shard_map/pallas_call | solution.py:382
  124.8 2.0 %collective-permute-done.11 = bf16[576,512]{1,0:T(8,128)(2,1)S(1)} collective-permute-done((bf16[576,512]{1,0:T(8,128)(2,1)S(1)}, bf16[576,512]{1,0:T(8,128)(2,1)S(1)}, u32[]{:S(2)}, u32[]{:S(2)}) %collective-permute-start.11) | collective-permute-done | bytes 589856 | tf_op jit(solution)/shard_map/ppermute | solution.py:578
  128.4 3.0 %collective-permute-start.12 = (bf16[144,512]{1,0:T(8,128)(2,1)S(1)}, bf16[144,512]{1,0:T(8,128)(2,1)S(1)}, u32[]{:S(2)}, u32[]{:S(2)}) collective-permute-start(bf16[144,512]{1,0:T(8,128)(2,1)S(1)} %get-tuple-element.109), channel_id=1, source_target_pairs={{0,6},{1,7},{2,4},{3,5},{4,2},{5,3},{6,0},{7,1},{8,14},{9,15},{10,... | collective-permute-start | bytes 442376 | tf_op jit(solution)/shard_map/ppermute | solution.py:578
  132.9 4.2 %collective-permute-done.12 = bf16[144,512]{1,0:T(8,128)(2,1)S(1)} collective-permute-done((bf16[144,512]{1,0:T(8,128)(2,1)S(1)}, bf16[144,512]{1,0:T(8,128)(2,1)S(1)}, u32[]{:S(2)}, u32[]{:S(2)}) %collective-permute-start.12) | collective-permute-done | bytes 147488 | tf_op jit(solution)/shard_map/ppermute | solution.py:578
  137.1 8.3 %collective-permute-done.13 = bf16[144,512]{1,0:T(8,128)(2,1)S(1)} collective-permute-done((bf16[144,512]{1,0:T(8,128)(2,1)S(1)}, bf16[144,512]{1,0:T(8,128)(2,1)S(1)}, u32[]{:S(2)}, u32[]{:S(2)}) %collective-permute-start.13) | collective-permute-done | bytes 147488 | tf_op jit(solution)/shard_map/ppermute | solution.py:578
  145.6 3.1 %collective-permute-start.16 = (bf16[144,512]{1,0:T(8,128)(2,1)S(1)}, bf16[144,512]{1,0:T(8,128)(2,1)S(1)}, u32[]{:S(2)}, u32[]{:S(2)}) collective-permute-start(bf16[144,512]{1,0:T(8,128)(2,1)S(1)} %add_convert_fusion.2.refs_0_), channel_id=1, source_target_pairs={{0,4},{1,5},{2,6},{3,7},{4,0},{5,1},{6,2},{7,3},{8,12},{9,13},{10,... | collective-permute-start | bytes 442376 | tf_op jit(solution)/shard_map/ppermute | solution.py:578
  150.0 3.4 %collective-permute-done.15.refs_1_ = bf16[144,512]{1,0:T(8,128)(2,1)S(1)} collective-permute-done((bf16[144,512]{1,0:T(8,128)(2,1)S(1)}, bf16[144,512]{1,0:T(8,128)(2,1)S(1)}, u32[]{:S(2)}, u32[]{:S(2)}) %collective-permute-start.15) | collective-permute-done | bytes 147488 | tf_op jit(solution)/shard_map/ppermute | solution.py:578
  153.6 4.0 %collective-permute-start.18 = (f32[2,256]{1,0:T(2,128)S(1)}, f32[2,256]{1,0:T(2,128)S(1)}, u32[]{:S(2)}, u32[]{:S(2)}) collective-permute-start(f32[2,256]{1,0:T(2,128)S(1)} %get-tuple-element.112), channel_id=1, source_target_pairs={{0,8},{8,0},{16,24},{24,16},{1,9},{9,1},{17,25},{25,17},{2,10},{10... | collective-permute-start | bytes 6152 | tf_op jit(solution)/shard_map/ppermute | solution.py:573
  157.6 1.9 %collective-permute-start.19 = (f32[2,256]{1,0:T(2,128)S(1)}, f32[2,256]{1,0:T(2,128)S(1)}, u32[]{:S(2)}, u32[]{:S(2)}) collective-permute-start(f32[2,256]{1,0:T(2,128)S(1)} %get-tuple-element.114), channel_id=1, source_target_pairs={{0,16},{8,24},{16,0},{24,8},{1,17},{9,25},{17,1},{25,9},{2,18},{10... | collective-permute-start | bytes 6152 | tf_op jit(solution)/shard_map/ppermute | solution.py:573
  162.0 2.0 %collective-permute-done.20 = f32[2,256]{1,0:T(2,128)S(1)} collective-permute-done((f32[2,256]{1,0:T(2,128)S(1)}, f32[2,256]{1,0:T(2,128)S(1)}, u32[]{:S(2)}, u32[]{:S(2)}) %collective-permute-start.20) | collective-permute-done | bytes 2080 | tf_op jit(solution)/shard_map/ppermute | solution.py:573
  164.6 2.0 %collective-permute-done.21.other = bf16[576,512]{1,0:T(8,128)(2,1)S(1)} collective-permute-done((bf16[576,512]{1,0:T(8,128)(2,1)S(1)}, bf16[576,512]{1,0:T(8,128)(2,1)S(1)}, u32[]{:S(2)}, u32[]{:S(2)}) %collective-permute-start.21) | collective-permute-done | bytes 589856 | tf_op jit(solution)/shard_map/ppermute | solution.py:578
  166.6 4.0 %shard_map.196 = (f32[771,4,128]{2,1,0:T(4,128)}, f32[1,512]{1,0:T(1,128)}, f32[1,512]{1,0:T(1,128)}, f32[512,512]{1,0:T(8,128)}, f32[1,512]{1,0:T(1,128)}, /*index=5*/f32[1,512]{1,0:T(1,128)}) custom-call(s32[3]{0:T(128)S(1)} %pad_add_fusion.sc, bf16[576,512]{1,0:T(8,128)(2,1)S(1)} %shard_map.195.mine, bf16[576,512]{1,0:T(8,128)(2,1)S(1)} %collective-permute-done.21.other, ...), custom_call_target="tpu_custom_call" | custom-call | flops 33554432 | bytes 4718592 | tf_op jit(solution)/shard_map/pallas_call | solution.py:558
  (66 shorter events, 20.5 us)
Async XLA Ops:
  4.0 8.0 %collective-permute-start = (bf16[144,512]{1,0:T(8,128)(2,1)}, bf16[144,512]{1,0:T(8,128)(2,1)S(1)}, u32[]{:S(2)}, u32[]{:S(2)}) collective-permute-start(bf16[144,512]{1,0:T(8,128)(2,1)} %get-tuple-element.51), channel_id=1, source_target_pairs={{0,24},{8,16},{16,8},{24,0},{1,25},{9,17},{17,9},{25,1},{2,26},{10... | collective-permute-start | bytes 442376 | tf_op jit(solution)/shard_map/ppermute | solution.py:573
  12.1 17.5 %collective-permute-start.1 = (bf16[576,512]{1,0:T(8,128)(2,1)}, bf16[576,512]{1,0:T(8,128)(2,1)S(1)}, u32[]{:S(2)}, u32[]{:S(2)}) collective-permute-start(bf16[576,512]{1,0:T(8,128)(2,1)} %get-tuple-element.56), channel_id=1, source_target_pairs={{0,8},{8,0},{16,24},{24,16},{1,9},{9,1},{17,25},{25,17},{2,10},{10... | collective-permute-start | bytes 1769480 | tf_op jit(solution)/shard_map/ppermute | solution.py:573
  13.7 15.8 %collective-permute-start.2 = (bf16[576,512]{1,0:T(8,128)(2,1)}, bf16[576,512]{1,0:T(8,128)(2,1)S(1)}, u32[]{:S(2)}, u32[]{:S(2)}) collective-permute-start(bf16[576,512]{1,0:T(8,128)(2,1)} %get-tuple-element.56), channel_id=1, source_target_pairs={{0,16},{8,24},{16,0},{24,8},{1,17},{9,25},{17,1},{25,9},{2,18},{10... | collective-permute-start | bytes 1769480 | tf_op jit(solution)/shard_map/ppermute | solution.py:573
  15.3 6.4 %collective-permute-start.3 = (bf16[144,512]{1,0:T(8,128)(2,1)S(1)}, bf16[144,512]{1,0:T(8,128)(2,1)S(1)}, u32[]{:S(2)}, u32[]{:S(2)}) collective-permute-start(bf16[144,512]{1,0:T(8,128)(2,1)S(1)} %collective-permute-done.refs_2_), channel_id=1, source_target_pairs={{0,2},{1,3},{2,0},{3,1},{4,6},{5,7},{6,4},{7,5},{8,10},{9,11},{10,... | collective-permute-start | bytes 442376 | tf_op jit(solution)/shard_map/ppermute | solution.py:578
  16.8 12.7 %collective-permute-start.4 = (bf16[144,512]{1,0:T(8,128)(2,1)S(1)}, bf16[144,512]{1,0:T(8,128)(2,1)S(1)}, u32[]{:S(2)}, u32[]{:S(2)}) collective-permute-start(bf16[144,512]{1,0:T(8,128)(2,1)S(1)} %collective-permute-done.refs_2_), channel_id=1, source_target_pairs={{0,4},{1,5},{2,6},{3,7},{4,0},{5,1},{6,2},{7,3},{8,12},{9,13},{10,... | collective-permute-start | bytes 442376 | tf_op jit(solution)/shard_map/ppermute | solution.py:578
  19.4 10.1 %collective-permute-start.5 = (bf16[144,512]{1,0:T(8,128)(2,1)S(1)}, bf16[144,512]{1,0:T(8,128)(2,1)S(1)}, u32[]{:S(2)}, u32[]{:S(2)}) collective-permute-start(bf16[144,512]{1,0:T(8,128)(2,1)S(1)} %collective-permute-done.refs_2_), channel_id=1, source_target_pairs={{0,6},{1,7},{2,4},{3,5},{4,2},{5,3},{6,0},{7,1},{8,14},{9,15},{10,... | collective-permute-start | bytes 442376 | tf_op jit(solution)/shard_map/ppermute | solution.py:578
  30.6 3.8 %collective-permute-start.6 = (bf16[1728,512]{1,0:T(8,128)(2,1)S(1)}, bf16[1728,512]{1,0:T(8,128)(2,1)S(1)}, u32[]{:S(2)}, u32[]{:S(2)}) collective-permute-start(bf16[1728,512]{1,0:T(8,128)(2,1)S(1)} %shard_map.188.refs_1_), channel_id=1, source_target_pairs={{0,1},{1,0},{2,3},{3,2},{4,5},{5,4},{6,7},{7,6},{8,9},{9,8},{10,11... | collective-permute-start | bytes 5308424 | tf_op jit(solution)/shard_map/ppermute | solution.py:578
  69.0 28.8 %collective-permute-start.10 = (bf16[1152,512]{1,0:T(8,128)(2,1)S(1)}, bf16[1152,512]{1,0:T(8,128)(2,1)S(1)}, u32[]{:S(2)}, u32[]{:S(2)}) collective-permute-start(bf16[1152,512]{1,0:T(8,128)(2,1)S(1)} %get-tuple-element.64), channel_id=1, source_target_pairs={{0,16},{8,24},{16,0},{24,8},{1,17},{9,25},{17,1},{25,9},{2,18},{10... | collective-permute-start | bytes 3538952 | tf_op jit(solution)/shard_map/ppermute | solution.py:573
  69.4 28.9 %collective-permute-start.9 = (bf16[1152,512]{1,0:T(8,128)(2,1)S(1)}, bf16[1152,512]{1,0:T(8,128)(2,1)S(1)}, u32[]{:S(2)}, u32[]{:S(2)}) collective-permute-start(bf16[1152,512]{1,0:T(8,128)(2,1)S(1)} %get-tuple-element.63), channel_id=1, source_target_pairs={{0,8},{8,0},{16,24},{24,16},{1,9},{9,1},{17,25},{25,17},{2,10},{10... | collective-permute-start | bytes 3538952 | tf_op jit(solution)/shard_map/ppermute | solution.py:573
  92.6 21.4 %collective-permute-start.7 = (bf16[768,512]{1,0:T(8,128)(2,1)S(1)}, bf16[768,512]{1,0:T(8,128)(2,1)S(1)}, u32[]{:S(2)}, u32[]{:S(2)}) collective-permute-start(bf16[768,512]{1,0:T(8,128)(2,1)S(1)} %get-tuple-element.60), channel_id=1, source_target_pairs={{0,8},{8,0},{16,24},{24,16},{1,9},{9,1},{17,25},{25,17},{2,10},{10... | collective-permute-start | bytes 2359304 | tf_op jit(solution)/shard_map/ppermute | solution.py:573
  92.6 21.4 %collective-permute-start.8 = (bf16[768,512]{1,0:T(8,128)(2,1)S(1)}, bf16[768,512]{1,0:T(8,128)(2,1)S(1)}, u32[]{:S(2)}, u32[]{:S(2)}) collective-permute-start(bf16[768,512]{1,0:T(8,128)(2,1)S(1)} %get-tuple-element.61), channel_id=1, source_target_pairs={{0,16},{8,24},{16,0},{24,8},{1,17},{9,25},{17,1},{25,9},{2,18},{10... | collective-permute-start | bytes 2359304 | tf_op jit(solution)/shard_map/ppermute | solution.py:573
  124.8 2.0 %collective-permute-start.11 = (bf16[576,512]{1,0:T(8,128)(2,1)S(1)}, bf16[576,512]{1,0:T(8,128)(2,1)S(1)}, u32[]{:S(2)}, u32[]{:S(2)}) collective-permute-start(bf16[576,512]{1,0:T(8,128)(2,1)S(1)} %add_convert_fusion.1), channel_id=1, source_target_pairs={{0,1},{1,0},{2,3},{3,2},{4,5},{5,4},{6,7},{7,6},{8,9},{9,8},{10,11... | collective-permute-start | bytes 1769480 | tf_op jit(solution)/shard_map/ppermute | solution.py:578
  128.4 38.2 %copy-start = (bf16[1,771,512]{2,1,0:T(8,128)(2,1)S(1)}, bf16[1,771,512]{2,1,0:T(8,128)(2,1)}, u32[]{:S(2)}) copy-start(bf16[1,771,512]{2,1,0:T(8,128)(2,1)} %param.17) | copy-start | bytes 2368516
  128.4 38.2 %copy-start.1 = (bf16[1,512,512]{2,1,0:T(8,128)(2,1)S(1)}, bf16[1,512,512]{2,1,0:T(8,128)(2,1)}, u32[]{:S(2)}) copy-start(bf16[1,512,512]{2,1,0:T(8,128)(2,1)} %param.20) | copy-start | bytes 1572868
  128.4 8.7 %collective-permute-start.12 = (bf16[144,512]{1,0:T(8,128)(2,1)S(1)}, bf16[144,512]{1,0:T(8,128)(2,1)S(1)}, u32[]{:S(2)}, u32[]{:S(2)}) collective-permute-start(bf16[144,512]{1,0:T(8,128)(2,1)S(1)} %get-tuple-element.109), channel_id=1, source_target_pairs={{0,6},{1,7},{2,4},{3,5},{4,2},{5,3},{6,0},{7,1},{8,14},{9,15},{10,... | collective-permute-start | bytes 442376 | tf_op jit(solution)/shard_map/ppermute | solution.py:578
  131.4 14.0 %collective-permute-start.13 = (bf16[144,512]{1,0:T(8,128)(2,1)S(1)}, bf16[144,512]{1,0:T(8,128)(2,1)S(1)}, u32[]{:S(2)}, u32[]{:S(2)}) collective-permute-start(bf16[144,512]{1,0:T(8,128)(2,1)S(1)} %get-tuple-element.111), channel_id=1, source_target_pairs={{0,4},{1,5},{2,6},{3,7},{4,0},{5,1},{6,2},{7,3},{8,12},{9,13},{10,... | collective-permute-start | bytes 442376 | tf_op jit(solution)/shard_map/ppermute | solution.py:578
  132.1 13.3 %collective-permute-start.14 = (bf16[144,512]{1,0:T(8,128)(2,1)S(1)}, bf16[144,512]{1,0:T(8,128)(2,1)S(1)}, u32[]{:S(2)}, u32[]{:S(2)}) collective-permute-start(bf16[144,512]{1,0:T(8,128)(2,1)S(1)} %get-tuple-element.110), channel_id=1, source_target_pairs={{0,2},{1,3},{2,0},{3,1},{4,6},{5,7},{6,4},{7,5},{8,10},{9,11},{10,... | collective-permute-start | bytes 442376 | tf_op jit(solution)/shard_map/ppermute | solution.py:578
  145.5 7.9 %collective-permute-start.15 = (bf16[144,512]{1,0:T(8,128)(2,1)S(1)}, bf16[144,512]{1,0:T(8,128)(2,1)S(1)}, u32[]{:S(2)}, u32[]{:S(2)}) collective-permute-start(bf16[144,512]{1,0:T(8,128)(2,1)S(1)} %add_convert_fusion.2.refs_0_), channel_id=1, source_target_pairs={{0,2},{1,3},{2,0},{3,1},{4,6},{5,7},{6,4},{7,5},{8,10},{9,11},{10,... | collective-permute-start | bytes 442376 | tf_op jit(solution)/shard_map/ppermute | solution.py:578
  145.6 15.3 %collective-permute-start.16 = (bf16[144,512]{1,0:T(8,128)(2,1)S(1)}, bf16[144,512]{1,0:T(8,128)(2,1)S(1)}, u32[]{:S(2)}, u32[]{:S(2)}) collective-permute-start(bf16[144,512]{1,0:T(8,128)(2,1)S(1)} %add_convert_fusion.2.refs_0_), channel_id=1, source_target_pairs={{0,4},{1,5},{2,6},{3,7},{4,0},{5,1},{6,2},{7,3},{8,12},{9,13},{10,... | collective-permute-start | bytes 442376 | tf_op jit(solution)/shard_map/ppermute | solution.py:578
  148.7 12.2 %collective-permute-start.17 = (bf16[144,512]{1,0:T(8,128)(2,1)S(1)}, bf16[144,512]{1,0:T(8,128)(2,1)S(1)}, u32[]{:S(2)}, u32[]{:S(2)}) collective-permute-start(bf16[144,512]{1,0:T(8,128)(2,1)S(1)} %add_convert_fusion.2.refs_0_), channel_id=1, source_target_pairs={{0,6},{1,7},{2,4},{3,5},{4,2},{5,3},{6,0},{7,1},{8,14},{9,15},{10,... | collective-permute-start | bytes 442376 | tf_op jit(solution)/shard_map/ppermute | solution.py:578
  153.6 8.4 %collective-permute-start.18 = (f32[2,256]{1,0:T(2,128)S(1)}, f32[2,256]{1,0:T(2,128)S(1)}, u32[]{:S(2)}, u32[]{:S(2)}) collective-permute-start(f32[2,256]{1,0:T(2,128)S(1)} %get-tuple-element.112), channel_id=1, source_target_pairs={{0,8},{8,0},{16,24},{24,16},{1,9},{9,1},{17,25},{25,17},{2,10},{10... | collective-permute-start | bytes 6152 | tf_op jit(solution)/shard_map/ppermute | solution.py:573
  157.6 4.4 %collective-permute-start.19 = (f32[2,256]{1,0:T(2,128)S(1)}, f32[2,256]{1,0:T(2,128)S(1)}, u32[]{:S(2)}, u32[]{:S(2)}) collective-permute-start(f32[2,256]{1,0:T(2,128)S(1)} %get-tuple-element.114), channel_id=1, source_target_pairs={{0,16},{8,24},{16,0},{24,8},{1,17},{9,25},{17,1},{25,9},{2,18},{10... | collective-permute-start | bytes 6152 | tf_op jit(solution)/shard_map/ppermute | solution.py:573
  159.5 4.5 %collective-permute-start.20 = (f32[2,256]{1,0:T(2,128)S(1)}, f32[2,256]{1,0:T(2,128)S(1)}, u32[]{:S(2)}, u32[]{:S(2)}) collective-permute-start(f32[2,256]{1,0:T(2,128)S(1)} %get-tuple-element.113), channel_id=1, source_target_pairs={{0,24},{8,16},{16,8},{24,0},{1,25},{9,17},{17,9},{25,1},{2,26},{10... | collective-permute-start | bytes 6152 | tf_op jit(solution)/shard_map/ppermute | solution.py:573
  164.6 2.0 %collective-permute-start.21 = (bf16[576,512]{1,0:T(8,128)(2,1)S(1)}, bf16[576,512]{1,0:T(8,128)(2,1)S(1)}, u32[]{:S(2)}, u32[]{:S(2)}) collective-permute-start(bf16[576,512]{1,0:T(8,128)(2,1)S(1)} %shard_map.195.mine), channel_id=1, source_target_pairs={{0,1},{1,0},{2,3},{3,2},{4,5},{5,4},{6,7},{7,6},{8,9},{9,8},{10,11... | collective-permute-start | bytes 1769480 | tf_op jit(solution)/shard_map/ppermute | solution.py:578
  (11 other events, 182.0 us)

commit v2 on v1

--- a/solution.py
+++ b/solution.py
@@ -147,7 +147,7 @@
 
 
 def self_kernel(
-    plan, steps, aliased, sc, h_in, g_in, ids, places, other_h, other_ids, other_places, cell_shape, weights, *refs
+    plan, steps, deep, aliased, sc, h_in, g_in, ids, places, other_h, other_ids, other_places, cell_shape, weights, *refs
 ):
     act, ig, give_x, give_y, after_first, mine, theirs, ext, ext_turned, states, mids, slope1, slope2, *accs = refs[aliased:]
     section, core = sc[0], sc[1]
@@ -162,13 +162,22 @@
         for acc in accs:
             acc[...] = jnp.zeros_like(acc)
 
-    @pl.when(section == 2)
+    other = lambda i: pl.ds(pl.multiple_of(step * rows + i * half, 128), half)
+
+    def ahead(k, source):
+        def keep(i, z):
+            after_first[other(i), :] = silu_parts(z)[0]
+        stream(2, do.inner(k, source), lambda i, z: silu_parts(z)[0], do.outer(k), keep)
+
+    @pl.when((section == 2) | (section == 1) if deep else section == 2)
     def _():
         place_cells(other_ids, other_places, cell_shape, plan, ext, ext_turned)
-
-        def keep(i, z):
-            after_first[pl.ds(pl.multiple_of(step * rows + i * half, 128), half), :] = silu_parts(z)[0]
-        stream(2, do.inner(0, lambda i: other_h[subs[i], :]), lambda i, z: silu_parts(z)[0], do.outer(0), keep)
+        ahead(0, lambda i: other_h[subs[i], :])
+
+    if deep:
+        @pl.when(section == 2)
+        def _():
+            ahead(1, lambda i: after_first[other(i), :])
 
     place_cells(ids, places, cell_shape, plan, ext, ext_turned)
     states[0] = h_in[...]
@@ -242,7 +251,7 @@
 
 
 def helped_kernel(
-    plan, steps, counts, sc, h_in, g_in, ids, places, cell_shape, weights, *refs
+    plan, steps, deep, counts, sc, h_in, g_in, ids, places, cell_shape, weights, *refs
 ):
     sources, refs = refs[: 3 * len(counts)], refs[3 * len(counts) + 2 :]
     act, ig, mine, theirs, ext, ext_turned, entering, got, mid, slope1, slope2, *accs = refs
@@ -271,11 +280,11 @@
             got[subs[0], :] = got_x[...]
             got[subs[1], :] = got_y[...]
 
-        @pl.when(now & (section == 2))
+        @pl.when(now & ((section == 2) | (section == 1) if deep else section == 2))
         def _():
             entering[...] = after_first[...]
 
-    @pl.when(section <= 1)
+    @pl.when((section == 0) if deep else (section <= 1))
     def _():
         entering[...] = h_in[...]
 
@@ -314,9 +323,10 @@
     def source(i):
         return entering[subs[i], :]
 
-    @pl.when((section == 1) | (section == 2))
-    def _():
-        stream(2, do.inner(section - 1, source), active_only, do.outer(section - 1), enter)
+    if not deep:
+        @pl.when((section == 1) | (section == 2))
+        def _():
+            stream(2, do.inner(section - 1, source), active_only, do.outer(section - 1), enter)
 
     stream(2, do.inner(section, source), keep_active, do.outer(section), keep_own,
            do.back_second(section, lambda i: slope2[subs[i], :]), inner_grad, do.back_first(section), enter_grad)
@@ -327,7 +337,7 @@
         store_weight_grads(accs, plan, core, mine, theirs)
 
 
-def run_blocks(plan, done, place, h, g, ids, places, cell_shape, weights, into, counts, sources):
+def run_blocks(plan, deep, done, place, h, g, ids, places, cell_shape, weights, into, counts, sources):
     total, width = h.shape
     blocks = total // ROWS
     helped = len(sources) > 0
@@ -338,7 +348,8 @@
         return (blocks // 2 - start if helped else start) + done + i
 
     def there(i, sc):
-        return jnp.where(sc[0] == 2, blocks // 2 - self_half(sc[0], blocks) + done + i, 0)
+        used = (sc[0] == 2) | (sc[0] == 1) if deep else sc[0] == 2
+        return jnp.where(used, blocks // 2 - self_half(sc[0], blocks) + done + i, 0)
 
     def block_specs(where):
         return [
@@ -354,7 +365,7 @@
     block = lambda *lead: pltpu.VMEM((*lead, ROWS, width), BF)
     scratch = [pltpu.VMEM((ROWS, plan.cells), BF), pltpu.VMEM((plan.cells, ROWS), BF)]
     if helped:
-        kernel = functools.partial(helped_kernel, plan, steps, counts)
+        kernel = functools.partial(helped_kernel, plan, steps, deep, counts)
         out_shape = [array(total)] * 2 + [array(plan.half)] * 2
         out_specs = [rows, rows, vmem, vmem]
         scratch += [block()] * 5
@@ -368,7 +379,7 @@
         in_specs = [rows, rows, *block_specs(here), vmem, vmem, *source_specs, hbm, hbm]
         units = 8
     else:
-        kernel = functools.partial(self_kernel, plan, steps, len(into))
+        kernel = functools.partial(self_kernel, plan, steps, deep, len(into))
         out_shape = ([array(total)] * 2 + [array(steps * ROWS // 2)] * 2 + [array(steps * ROWS)]
                      + [array(plan.half)] * 2)
         out_specs = [rows, rows, *[vmem] * 5]
@@ -630,9 +641,9 @@
     same = (inputs, cotangent, ids, places, cell_shape, weights)
     given, parts, into, starts = [], [], [], []
     done = 0
-    for steps in CALLS:
+    for turn, steps in enumerate(CALLS):
         *into, give_x, give_y, after_first, mine, theirs = run_blocks(
-            plan, done, place, *same, into, (steps,), []
+            plan, turn > 0, done, place, *same, into, (steps,), []
         )
         given.append((swap_section(give_x, 1), swap_section(give_y, 2), after_first))
         parts.append((mine, theirs))
@@ -641,7 +652,7 @@
     for calls in HELPED_CALLS:
         sources = [source for call in calls for source in given[call]]
         counts = tuple(CALLS[call] for call in calls)
-        *into, mine, theirs = run_blocks(plan, starts[calls[0]], place, *same, into, counts, sources)
+        *into, mine, theirs = run_blocks(plan, calls[0] > 0, starts[calls[0]], place, *same, into, counts, sources)
         parts.append((mine, theirs))
     act, ig = into
 

time: 172 us -> 169 us (0.983)
    ppermute x10, waiting for transfers between devices: 12.1 us -> 9.23 us  [swap_section(): return lax.ppermute(block, 'section', route)]
    ppermute x12, waiting for transfers between devices: 31.6 us -> 33.9 us  [swap_dp(): return lax.ppermute(block, 'dp', route)]
  transfers between devices with their start and end apart: 22 -> 22, of which waited for: 13 -> 15; matrix products, arithmetic and copies ran while one was open for 0% -> 0% of each run, Pallas kernels for 23% -> 23%
where the time goes in v2:
time: 169 us
  Pallas kernels  92.5 us (55%)
  waiting for transfers between devices  43.1 us (26%)
  starting transfers between devices  28.7 us (17%)
  other arithmetic  2.52 us (1%)
    pallas_call x4, Pallas kernels, run_blocks(): pl.pallas_call(kernel, grid_spec=pltpu.PrefetchScalarGridSpec(num_scalar_...  79.8 us
    ppermute x12, waiting for transfers between devices, swap_dp(): return lax.ppermute(block, 'dp', route)  33.9 us
    ppermute x10, starting transfers between devices, swap_section(): return lax.ppermute(block, 'section', route)  15.4 us
    ppermute x12, starting transfers between devices, swap_dp(): return lax.ppermute(block, 'dp', route)  13.3 us
    ppermute x10, waiting for transfers between devices, swap_section(): return lax.ppermute(block, 'section', route)  9.23 us
    pallas_call x1, Pallas kernels, finish_grads(): pl.pallas_call(functools.partial(grads_kernel, plan, latents.shape[1]), g...  3.99 us
    pallas_call x2, Pallas kernels, spread_weights(): pl.pallas_call(functools.partial(spread_kernel, plan, near), grid_spec=pl...  3.49 us
  transfers between devices with their start and end apart: 22, of which 15 were waited for; matrix products, arithmetic and copies ran while one was open for 0% of the time, Pallas kernels for 23%

profile of v2, /device:TPU:0, one launch (start us, length us, event | category | flops | bytes accessed | tf_op | source)
XLA Modules:
  0.0 168.6 jit_solution(17757221973076777962)
XLA Ops:
  0.7 3.4 %shard_map.187 = (bf16[1152,512]{1,0:T(8,128)(2,1)}, bf16[256,512]{1,0:T(8,128)(2,1)}, bf16[576,512]{1,0:T(8,128)(2,1)}, bf16[144,512]{1,0:T(8,128)(2,1)}) custom-call(bf16[771,512]{1,0:T(8,128)(2,1)} %bitcast.15, bf16[1,512]{1,0:T(2,128)(2,1)} %gain_first.1, bf16[1,512]{1,0:T(2,128)(2,1)} %refs_2_.1, bf16[512,512]{1,0:T(8,128)(2,1)} %bitcast.17, ...), custom_call_target="tpu_custom_call" | custom-call | flops 33554432 | bytes 2359296 | tf_op jit(solution)/shard_map/pallas_call | solution.py:449
  4.0 4.0 %collective-permute-start = (bf16[144,512]{1,0:T(8,128)(2,1)}, bf16[144,512]{1,0:T(8,128)(2,1)S(1)}, u32[]{:S(2)}, u32[]{:S(2)}) collective-permute-start(bf16[144,512]{1,0:T(8,128)(2,1)} %get-tuple-element.51), channel_id=1, source_target_pairs={{0,24},{8,16},{16,8},{24,0},{1,25},{9,17},{17,9},{25,1},{2,26},{10... | collective-permute-start | bytes 442376 | tf_op jit(solution)/shard_map/ppermute | solution.py:584
  8.1 3.9 %collective-permute-done.refs_2_ = bf16[144,512]{1,0:T(8,128)(2,1)S(1)} collective-permute-done((bf16[144,512]{1,0:T(8,128)(2,1)}, bf16[144,512]{1,0:T(8,128)(2,1)S(1)}, u32[]{:S(2)}, u32[]{:S(2)}) %collective-permute-start) | collective-permute-done | bytes 147488 | tf_op jit(solution)/shard_map/ppermute | solution.py:584
  16.8 2.6 %collective-permute-start.4 = (bf16[144,512]{1,0:T(8,128)(2,1)S(1)}, bf16[144,512]{1,0:T(8,128)(2,1)S(1)}, u32[]{:S(2)}, u32[]{:S(2)}) collective-permute-start(bf16[144,512]{1,0:T(8,128)(2,1)S(1)} %collective-permute-done.refs_2_), channel_id=1, source_target_pairs={{0,4},{1,5},{2,6},{3,7},{4,0},{5,1},{6,2},{7,3},{8,12},{9,13},{10,... | collective-permute-start | bytes 442376 | tf_op jit(solution)/shard_map/ppermute | solution.py:589
  19.7 2.0 %collective-permute-done.3.refs_3_ = bf16[144,512]{1,0:T(8,128)(2,1)S(1)} collective-permute-done((bf16[144,512]{1,0:T(8,128)(2,1)S(1)}, bf16[144,512]{1,0:T(8,128)(2,1)S(1)}, u32[]{:S(2)}, u32[]{:S(2)}) %collective-permute-start.3) | collective-permute-done | bytes 147488 | tf_op jit(solution)/shard_map/ppermute | solution.py:589
  21.7 7.8 %collective-permute-done.4.refs_4_ = bf16[144,512]{1,0:T(8,128)(2,1)S(1)} collective-permute-done((bf16[144,512]{1,0:T(8,128)(2,1)S(1)}, bf16[144,512]{1,0:T(8,128)(2,1)S(1)}, u32[]{:S(2)}, u32[]{:S(2)}) %collective-permute-start.4) | collective-permute-done | bytes 147488 | tf_op jit(solution)/shard_map/ppermute | solution.py:589
  30.7 1.9 %shard_map.189.refs_0_ = bf16[4,1152,512]{2,1,0:T(8,128)(2,1)S(1)} custom-call(s32[3]{0:T(128)S(1)} %pad_add_fusion.sc, bf16[1152,512]{1,0:T(8,128)(2,1)S(1)} %copy-done.2, bf16[1728,512]{1,0:T(8,128)(2,1)S(1)} %shard_map.188.refs_1_), custom_call_target="tpu_custom_call" | custom-call | bytes 4718592 | tf_op jit(solution)/shard_map/pallas_call | solution.py:510
  36.0 33.0 %shard_map.191 = (bf16[7680,512]{1,0:T(8,128)(2,1)}, bf16[7680,512]{1,0:T(8,128)(2,1)}, bf16[1152,512]{1,0:T(8,128)(2,1)S(1)}, bf16[1152,512]{1,0:T(8,128)(2,1)S...) custom-call(s32[3]{0:T(128)S(1)} %pad_add_fusion.sc, ...), custom_call_target="tpu_custom_call" | custom-call | flops 25367150592 | bytes 14155776 | tf_op jit(solution)/shard_map/pallas_call | solution.py:393
  69.4 23.2 %shard_map.192 = (bf16[7680,512]{1,0:T(8,128)(2,1)}, bf16[7680,512]{1,0:T(8,128)(2,1)}, bf16[768,512]{1,0:T(8,128)(2,1)S(1)}, bf16[768,512]{1,0:T(8,128)(2,1)S(1...) custom-call(s32[3]{0:T(128)S(1)} %pad_add_fusion.sc, ...), custom_call_target="tpu_custom_call", output_to_operand_aliasing={{0}: (10, {}), {1}: (11, {})} | custom-call | flops 16911433728 | bytes 9437184 | tf_op jit(solution)/shard_map/pallas_call | solution.py:393
  92.6 2.7 %collective-permute-start.7 = (bf16[768,512]{1,0:T(8,128)(2,1)S(1)}, bf16[768,512]{1,0:T(8,128)(2,1)S(1)}, u32[]{:S(2)}, u32[]{:S(2)}) collective-permute-start(bf16[768,512]{1,0:T(8,128)(2,1)S(1)} %get-tuple-element.60), channel_id=1, source_target_pairs={{0,8},{8,0},{16,24},{24,16},{1,9},{9,1},{17,25},{25,17},{2,10},{10... | collective-permute-start | bytes 2359304 | tf_op jit(solution)/shard_map/ppermute | solution.py:584
  98.3 13.7 %shard_map.193 = (bf16[7680,512]{1,0:T(8,128)(2,1)}, bf16[7680,512]{1,0:T(8,128)(2,1)}, bf16[576,512]{1,0:T(8,128)(2,1)S(1)}, bf16[576,512]{1,0:T(8,128)(2,1)S(1)}) custom-call(s32[3]{0:T(128)S(1)} %pad_add_fusion.sc, bf16[7680,512]{1,0:T(8,128)(2,1)S(1)} %bitcast.14, bf16[7680,512]{1,0:T(8,128)(2,1)} %g_in.7, ...), custom_call_target="tpu_custom_call", output_to_operand_aliasing={{0}: (10, {}), {1}: (11, {})} | custom-call | flops 9663676416 | bytes 14155776 | tf_op jit(solution)/shard_map/pallas_call | solution.py:393
  112.0 2.0 %collective-permute-done.7.refs_0_ = bf16[768,512]{1,0:T(8,128)(2,1)S(1)} collective-permute-done((bf16[768,512]{1,0:T(8,128)(2,1)S(1)}, bf16[768,512]{1,0:T(8,128)(2,1)S(1)}, u32[]{:S(2)}, u32[]{:S(2)}) %collective-permute-start.7) | collective-permute-done | bytes 786464 | tf_op jit(solution)/shard_map/ppermute | solution.py:584
  114.1 10.0 %shard_map.194 = (bf16[7680,512]{1,0:T(8,128)(2,1)}, bf16[7680,512]{1,0:T(8,128)(2,1)}, bf16[576,512]{1,0:T(8,128)(2,1)S(1)}, bf16[576,512]{1,0:T(8,128)(2,1)S(1)}) custom-call(s32[3]{0:T(128)S(1)} %pad_add_fusion.sc, bf16[7680,512]{1,0:T(8,128)(2,1)S(1)} %bitcast.14, bf16[7680,512]{1,0:T(8,128)(2,1)} %g_in.7, ...), custom_call_target="tpu_custom_call", output_to_operand_aliasing={{0}: (10, {}), {1}: (11, {})} | custom-call | flops 6442450944 | bytes 9437184 | tf_op jit(solution)/shard_map/pallas_call | solution.py:393
  124.9 2.0 %collective-permute-done.11 = bf16[576,512]{1,0:T(8,128)(2,1)S(1)} collective-permute-done((bf16[576,512]{1,0:T(8,128)(2,1)S(1)}, bf16[576,512]{1,0:T(8,128)(2,1)S(1)}, u32[]{:S(2)}, u32[]{:S(2)}) %collective-permute-start.11) | collective-permute-done | bytes 589856 | tf_op jit(solution)/shard_map/ppermute | solution.py:589
  128.5 2.9 %collective-permute-start.12 = (bf16[144,512]{1,0:T(8,128)(2,1)S(1)}, bf16[144,512]{1,0:T(8,128)(2,1)S(1)}, u32[]{:S(2)}, u32[]{:S(2)}) collective-permute-start(bf16[144,512]{1,0:T(8,128)(2,1)S(1)} %get-tuple-element.109), channel_id=1, source_target_pairs={{0,6},{1,7},{2,4},{3,5},{4,2},{5,3},{6,0},{7,1},{8,14},{9,15},{10,... | collective-permute-start | bytes 442376 | tf_op jit(solution)/shard_map/ppermute | solution.py:589
  132.9 4.2 %collective-permute-done.12 = bf16[144,512]{1,0:T(8,128)(2,1)S(1)} collective-permute-done((bf16[144,512]{1,0:T(8,128)(2,1)S(1)}, bf16[144,512]{1,0:T(8,128)(2,1)S(1)}, u32[]{:S(2)}, u32[]{:S(2)}) %collective-permute-start.12) | collective-permute-done | bytes 147488 | tf_op jit(solution)/shard_map/ppermute | solution.py:589
  137.1 8.3 %collective-permute-done.13 = bf16[144,512]{1,0:T(8,128)(2,1)S(1)} collective-permute-done((bf16[144,512]{1,0:T(8,128)(2,1)S(1)}, bf16[144,512]{1,0:T(8,128)(2,1)S(1)}, u32[]{:S(2)}, u32[]{:S(2)}) %collective-permute-start.13) | collective-permute-done | bytes 147488 | tf_op jit(solution)/shard_map/ppermute | solution.py:589
  145.7 3.0 %collective-permute-start.16 = (bf16[144,512]{1,0:T(8,128)(2,1)S(1)}, bf16[144,512]{1,0:T(8,128)(2,1)S(1)}, u32[]{:S(2)}, u32[]{:S(2)}) collective-permute-start(bf16[144,512]{1,0:T(8,128)(2,1)S(1)} %add_convert_fusion.2.refs_0_), channel_id=1, source_target_pairs={{0,4},{1,5},{2,6},{3,7},{4,0},{5,1},{6,2},{7,3},{8,12},{9,13},{10,... | collective-permute-start | bytes 442376 | tf_op jit(solution)/shard_map/ppermute | solution.py:589
  150.0 3.5 %collective-permute-done.15.refs_1_ = bf16[144,512]{1,0:T(8,128)(2,1)S(1)} collective-permute-done((bf16[144,512]{1,0:T(8,128)(2,1)S(1)}, bf16[144,512]{1,0:T(8,128)(2,1)S(1)}, u32[]{:S(2)}, u32[]{:S(2)}) %collective-permute-start.15) | collective-permute-done | bytes 147488 | tf_op jit(solution)/shard_map/ppermute | solution.py:589
  153.7 2.0 %collective-permute-start.18 = (f32[2,256]{1,0:T(2,128)S(1)}, f32[2,256]{1,0:T(2,128)S(1)}, u32[]{:S(2)}, u32[]{:S(2)}) collective-permute-start(f32[2,256]{1,0:T(2,128)S(1)} %get-tuple-element.112), channel_id=1, source_target_pairs={{0,8},{8,0},{16,24},{24,16},{1,9},{9,1},{17,25},{25,17},{2,10},{10... | collective-permute-start | bytes 6152 | tf_op jit(solution)/shard_map/ppermute | solution.py:584
  155.7 1.9 %collective-permute-start.19 = (f32[2,256]{1,0:T(2,128)S(1)}, f32[2,256]{1,0:T(2,128)S(1)}, u32[]{:S(2)}, u32[]{:S(2)}) collective-permute-start(f32[2,256]{1,0:T(2,128)S(1)} %get-tuple-element.114), channel_id=1, source_target_pairs={{0,16},{8,24},{16,0},{24,8},{1,17},{9,25},{17,1},{25,9},{2,18},{10... | collective-permute-start | bytes 6152 | tf_op jit(solution)/shard_map/ppermute | solution.py:584
  157.5 2.2 %collective-permute-done.16.refs_2_ = bf16[144,512]{1,0:T(8,128)(2,1)S(1)} collective-permute-done((bf16[144,512]{1,0:T(8,128)(2,1)S(1)}, bf16[144,512]{1,0:T(8,128)(2,1)S(1)}, u32[]{:S(2)}, u32[]{:S(2)}) %collective-permute-start.16) | collective-permute-done | bytes 147488 | tf_op jit(solution)/shard_map/ppermute | solution.py:589
  162.6 2.0 %collective-permute-done.21.other = bf16[576,512]{1,0:T(8,128)(2,1)S(1)} collective-permute-done((bf16[576,512]{1,0:T(8,128)(2,1)S(1)}, bf16[576,512]{1,0:T(8,128)(2,1)S(1)}, u32[]{:S(2)}, u32[]{:S(2)}) %collective-permute-start.21) | collective-permute-done | bytes 589856 | tf_op jit(solution)/shard_map/ppermute | solution.py:589
  164.6 4.0 %shard_map.196 = (f32[771,4,128]{2,1,0:T(4,128)}, f32[1,512]{1,0:T(1,128)}, f32[1,512]{1,0:T(1,128)}, f32[512,512]{1,0:T(8,128)}, f32[1,512]{1,0:T(1,128)}, /*index=5*/f32[1,512]{1,0:T(1,128)}) custom-call(s32[3]{0:T(128)S(1)} %pad_add_fusion.sc, bf16[576,512]{1,0:T(8,128)(2,1)S(1)} %shard_map.195.mine, bf16[576,512]{1,0:T(8,128)(2,1)S(1)} %collective-permute-done.21.other, ...), custom_call_target="tpu_custom_call" | custom-call | flops 33554432 | bytes 4718592 | tf_op jit(solution)/shard_map/pallas_call | solution.py:569
  (66 shorter events, 21.5 us)
Async XLA Ops:
  4.0 8.0 %collective-permute-start = (bf16[144,512]{1,0:T(8,128)(2,1)}, bf16[144,512]{1,0:T(8,128)(2,1)S(1)}, u32[]{:S(2)}, u32[]{:S(2)}) collective-permute-start(bf16[144,512]{1,0:T(8,128)(2,1)} %get-tuple-element.51), channel_id=1, source_target_pairs={{0,24},{8,16},{16,8},{24,0},{1,25},{9,17},{17,9},{25,1},{2,26},{10... | collective-permute-start | bytes 442376 | tf_op jit(solution)/shard_map/ppermute | solution.py:584
  12.1 17.5 %collective-permute-start.1 = (bf16[576,512]{1,0:T(8,128)(2,1)}, bf16[576,512]{1,0:T(8,128)(2,1)S(1)}, u32[]{:S(2)}, u32[]{:S(2)}) collective-permute-start(bf16[576,512]{1,0:T(8,128)(2,1)} %get-tuple-element.56), channel_id=1, source_target_pairs={{0,8},{8,0},{16,24},{24,16},{1,9},{9,1},{17,25},{25,17},{2,10},{10... | collective-permute-start | bytes 1769480 | tf_op jit(solution)/shard_map/ppermute | solution.py:584
  13.7 15.8 %collective-permute-start.2 = (bf16[576,512]{1,0:T(8,128)(2,1)}, bf16[576,512]{1,0:T(8,128)(2,1)S(1)}, u32[]{:S(2)}, u32[]{:S(2)}) collective-permute-start(bf16[576,512]{1,0:T(8,128)(2,1)} %get-tuple-element.56), channel_id=1, source_target_pairs={{0,16},{8,24},{16,0},{24,8},{1,17},{9,25},{17,1},{25,9},{2,18},{10... | collective-permute-start | bytes 1769480 | tf_op jit(solution)/shard_map/ppermute | solution.py:584
  15.3 6.4 %collective-permute-start.3 = (bf16[144,512]{1,0:T(8,128)(2,1)S(1)}, bf16[144,512]{1,0:T(8,128)(2,1)S(1)}, u32[]{:S(2)}, u32[]{:S(2)}) collective-permute-start(bf16[144,512]{1,0:T(8,128)(2,1)S(1)} %collective-permute-done.refs_2_), channel_id=1, source_target_pairs={{0,2},{1,3},{2,0},{3,1},{4,6},{5,7},{6,4},{7,5},{8,10},{9,11},{10,... | collective-permute-start | bytes 442376 | tf_op jit(solution)/shard_map/ppermute | solution.py:589
  16.8 12.7 %collective-permute-start.4 = (bf16[144,512]{1,0:T(8,128)(2,1)S(1)}, bf16[144,512]{1,0:T(8,128)(2,1)S(1)}, u32[]{:S(2)}, u32[]{:S(2)}) collective-permute-start(bf16[144,512]{1,0:T(8,128)(2,1)S(1)} %collective-permute-done.refs_2_), channel_id=1, source_target_pairs={{0,4},{1,5},{2,6},{3,7},{4,0},{5,1},{6,2},{7,3},{8,12},{9,13},{10,... | collective-permute-start | bytes 442376 | tf_op jit(solution)/shard_map/ppermute | solution.py:589
  19.4 10.1 %collective-permute-start.5 = (bf16[144,512]{1,0:T(8,128)(2,1)S(1)}, bf16[144,512]{1,0:T(8,128)(2,1)S(1)}, u32[]{:S(2)}, u32[]{:S(2)}) collective-permute-start(bf16[144,512]{1,0:T(8,128)(2,1)S(1)} %collective-permute-done.refs_2_), channel_id=1, source_target_pairs={{0,6},{1,7},{2,4},{3,5},{4,2},{5,3},{6,0},{7,1},{8,14},{9,15},{10,... | collective-permute-start | bytes 442376 | tf_op jit(solution)/shard_map/ppermute | solution.py:589
  30.6 3.8 %collective-permute-start.6 = (bf16[1728,512]{1,0:T(8,128)(2,1)S(1)}, bf16[1728,512]{1,0:T(8,128)(2,1)S(1)}, u32[]{:S(2)}, u32[]{:S(2)}) collective-permute-start(bf16[1728,512]{1,0:T(8,128)(2,1)S(1)} %shard_map.188.refs_1_), channel_id=1, source_target_pairs={{0,1},{1,0},{2,3},{3,2},{4,5},{5,4},{6,7},{7,6},{8,9},{9,8},{10,11... | collective-permute-start | bytes 5308424 | tf_op jit(solution)/shard_map/ppermute | solution.py:589
  69.0 28.0 %collective-permute-start.10 = (bf16[1152,512]{1,0:T(8,128)(2,1)S(1)}, bf16[1152,512]{1,0:T(8,128)(2,1)S(1)}, u32[]{:S(2)}, u32[]{:S(2)}) collective-permute-start(bf16[1152,512]{1,0:T(8,128)(2,1)S(1)} %get-tuple-element.64), channel_id=1, source_target_pairs={{0,16},{8,24},{16,0},{24,8},{1,17},{9,25},{17,1},{25,9},{2,18},{10... | collective-permute-start | bytes 3538952 | tf_op jit(solution)/shard_map/ppermute | solution.py:584
  69.4 28.9 %collective-permute-start.9 = (bf16[1152,512]{1,0:T(8,128)(2,1)S(1)}, bf16[1152,512]{1,0:T(8,128)(2,1)S(1)}, u32[]{:S(2)}, u32[]{:S(2)}) collective-permute-start(bf16[1152,512]{1,0:T(8,128)(2,1)S(1)} %get-tuple-element.63), channel_id=1, source_target_pairs={{0,8},{8,0},{16,24},{24,16},{1,9},{9,1},{17,25},{25,17},{2,10},{10... | collective-permute-start | bytes 3538952 | tf_op jit(solution)/shard_map/ppermute | solution.py:584
  92.6 21.4 %collective-permute-start.7 = (bf16[768,512]{1,0:T(8,128)(2,1)S(1)}, bf16[768,512]{1,0:T(8,128)(2,1)S(1)}, u32[]{:S(2)}, u32[]{:S(2)}) collective-permute-start(bf16[768,512]{1,0:T(8,128)(2,1)S(1)} %get-tuple-element.60), channel_id=1, source_target_pairs={{0,8},{8,0},{16,24},{24,16},{1,9},{9,1},{17,25},{25,17},{2,10},{10... | collective-permute-start | bytes 2359304 | tf_op jit(solution)/shard_map/ppermute | solution.py:584
  95.2 18.8 %collective-permute-start.8 = (bf16[768,512]{1,0:T(8,128)(2,1)S(1)}, bf16[768,512]{1,0:T(8,128)(2,1)S(1)}, u32[]{:S(2)}, u32[]{:S(2)}) collective-permute-start(bf16[768,512]{1,0:T(8,128)(2,1)S(1)} %get-tuple-element.61), channel_id=1, source_target_pairs={{0,16},{8,24},{16,0},{24,8},{1,17},{9,25},{17,1},{25,9},{2,18},{10... | collective-permute-start | bytes 2359304 | tf_op jit(solution)/shard_map/ppermute | solution.py:584
  124.9 2.0 %collective-permute-start.11 = (bf16[576,512]{1,0:T(8,128)(2,1)S(1)}, bf16[576,512]{1,0:T(8,128)(2,1)S(1)}, u32[]{:S(2)}, u32[]{:S(2)}) collective-permute-start(bf16[576,512]{1,0:T(8,128)(2,1)S(1)} %add_convert_fusion.1), channel_id=1, source_target_pairs={{0,1},{1,0},{2,3},{3,2},{4,5},{5,4},{6,7},{7,6},{8,9},{9,8},{10,11... | collective-permute-start | bytes 1769480 | tf_op jit(solution)/shard_map/ppermute | solution.py:589
  128.4 36.2 %copy-start = (bf16[1,771,512]{2,1,0:T(8,128)(2,1)S(1)}, bf16[1,771,512]{2,1,0:T(8,128)(2,1)}, u32[]{:S(2)}) copy-start(bf16[1,771,512]{2,1,0:T(8,128)(2,1)} %param.17) | copy-start | bytes 2368516
  128.4 36.2 %copy-start.1 = (bf16[1,512,512]{2,1,0:T(8,128)(2,1)S(1)}, bf16[1,512,512]{2,1,0:T(8,128)(2,1)}, u32[]{:S(2)}) copy-start(bf16[1,512,512]{2,1,0:T(8,128)(2,1)} %param.20) | copy-start | bytes 1572868
  128.5 8.7 %collective-permute-start.12 = (bf16[144,512]{1,0:T(8,128)(2,1)S(1)}, bf16[144,512]{1,0:T(8,128)(2,1)S(1)}, u32[]{:S(2)}, u32[]{:S(2)}) collective-permute-start(bf16[144,512]{1,0:T(8,128)(2,1)S(1)} %get-tuple-element.109), channel_id=1, source_target_pairs={{0,6},{1,7},{2,4},{3,5},{4,2},{5,3},{6,0},{7,1},{8,14},{9,15},{10,... | collective-permute-start | bytes 442376 | tf_op jit(solution)/shard_map/ppermute | solution.py:589
  131.4 14.1 %collective-permute-start.13 = (bf16[144,512]{1,0:T(8,128)(2,1)S(1)}, bf16[144,512]{1,0:T(8,128)(2,1)S(1)}, u32[]{:S(2)}, u32[]{:S(2)}) collective-permute-start(bf16[144,512]{1,0:T(8,128)(2,1)S(1)} %get-tuple-element.111), channel_id=1, source_target_pairs={{0,4},{1,5},{2,6},{3,7},{4,0},{5,1},{6,2},{7,3},{8,12},{9,13},{10,... | collective-permute-start | bytes 442376 | tf_op jit(solution)/shard_map/ppermute | solution.py:589
  132.1 13.3 %collective-permute-start.14 = (bf16[144,512]{1,0:T(8,128)(2,1)S(1)}, bf16[144,512]{1,0:T(8,128)(2,1)S(1)}, u32[]{:S(2)}, u32[]{:S(2)}) collective-permute-start(bf16[144,512]{1,0:T(8,128)(2,1)S(1)} %get-tuple-element.110), channel_id=1, source_target_pairs={{0,2},{1,3},{2,0},{3,1},{4,6},{5,7},{6,4},{7,5},{8,10},{9,11},{10,... | collective-permute-start | bytes 442376 | tf_op jit(solution)/shard_map/ppermute | solution.py:589
  145.6 7.9 %collective-permute-start.15 = (bf16[144,512]{1,0:T(8,128)(2,1)S(1)}, bf16[144,512]{1,0:T(8,128)(2,1)S(1)}, u32[]{:S(2)}, u32[]{:S(2)}) collective-permute-start(bf16[144,512]{1,0:T(8,128)(2,1)S(1)} %add_convert_fusion.2.refs_0_), channel_id=1, source_target_pairs={{0,2},{1,3},{2,0},{3,1},{4,6},{5,7},{6,4},{7,5},{8,10},{9,11},{10,... | collective-permute-start | bytes 442376 | tf_op jit(solution)/shard_map/ppermute | solution.py:589
  145.7 14.1 %collective-permute-start.16 = (bf16[144,512]{1,0:T(8,128)(2,1)S(1)}, bf16[144,512]{1,0:T(8,128)(2,1)S(1)}, u32[]{:S(2)}, u32[]{:S(2)}) collective-permute-start(bf16[144,512]{1,0:T(8,128)(2,1)S(1)} %add_convert_fusion.2.refs_0_), channel_id=1, source_target_pairs={{0,4},{1,5},{2,6},{3,7},{4,0},{5,1},{6,2},{7,3},{8,12},{9,13},{10,... | collective-permute-start | bytes 442376 | tf_op jit(solution)/shard_map/ppermute | solution.py:589
  148.7 11.1 %collective-permute-start.17 = (bf16[144,512]{1,0:T(8,128)(2,1)S(1)}, bf16[144,512]{1,0:T(8,128)(2,1)S(1)}, u32[]{:S(2)}, u32[]{:S(2)}) collective-permute-start(bf16[144,512]{1,0:T(8,128)(2,1)S(1)} %add_convert_fusion.2.refs_0_), channel_id=1, source_target_pairs={{0,6},{1,7},{2,4},{3,5},{4,2},{5,3},{6,0},{7,1},{8,14},{9,15},{10,... | collective-permute-start | bytes 442376 | tf_op jit(solution)/shard_map/ppermute | solution.py:589
  153.7 6.9 %collective-permute-start.18 = (f32[2,256]{1,0:T(2,128)S(1)}, f32[2,256]{1,0:T(2,128)S(1)}, u32[]{:S(2)}, u32[]{:S(2)}) collective-permute-start(f32[2,256]{1,0:T(2,128)S(1)} %get-tuple-element.112), channel_id=1, source_target_pairs={{0,8},{8,0},{16,24},{24,16},{1,9},{9,1},{17,25},{25,17},{2,10},{10... | collective-permute-start | bytes 6152 | tf_op jit(solution)/shard_map/ppermute | solution.py:584
  155.7 4.9 %collective-permute-start.19 = (f32[2,256]{1,0:T(2,128)S(1)}, f32[2,256]{1,0:T(2,128)S(1)}, u32[]{:S(2)}, u32[]{:S(2)}) collective-permute-start(f32[2,256]{1,0:T(2,128)S(1)} %get-tuple-element.114), channel_id=1, source_target_pairs={{0,16},{8,24},{16,0},{24,8},{1,17},{9,25},{17,1},{25,9},{2,18},{10... | collective-permute-start | bytes 6152 | tf_op jit(solution)/shard_map/ppermute | solution.py:584
  157.5 4.5 %collective-permute-start.20 = (f32[2,256]{1,0:T(2,128)S(1)}, f32[2,256]{1,0:T(2,128)S(1)}, u32[]{:S(2)}, u32[]{:S(2)}) collective-permute-start(f32[2,256]{1,0:T(2,128)S(1)} %get-tuple-element.113), channel_id=1, source_target_pairs={{0,24},{8,16},{16,8},{24,0},{1,25},{9,17},{17,9},{25,1},{2,26},{10... | collective-permute-start | bytes 6152 | tf_op jit(solution)/shard_map/ppermute | solution.py:584
  162.6 2.0 %collective-permute-start.21 = (bf16[576,512]{1,0:T(8,128)(2,1)S(1)}, bf16[576,512]{1,0:T(8,128)(2,1)S(1)}, u32[]{:S(2)}, u32[]{:S(2)}) collective-permute-start(bf16[576,512]{1,0:T(8,128)(2,1)S(1)} %shard_map.195.mine), channel_id=1, source_target_pairs={{0,1},{1,0},{2,3},{3,2},{4,5},{5,4},{6,7},{7,6},{8,9},{9,8},{10,11... | collective-permute-start | bytes 1769480 | tf_op jit(solution)/shard_map/ppermute | solution.py:589
  (11 other events, 176.0 us)

commit v3 on v2

--- a/solution.py
+++ b/solution.py
@@ -629,8 +629,8 @@
     ids = shape_ids.reshape(blocks, 1, ROWS)
     places = positions.reshape(coords, blocks, ROWS).transpose(1, 0, 2)
     far = swap_section(far, 3)
+    x_mine = swap_section(sending, 1)
     sending, far, ids, places, place = lax.optimization_barrier((sending, far, ids, places, place))
-    x_mine = swap_section(sending, 1)
     y_mine = swap_section(sending, 2)
     far_mine = gather_chips(plan, far)
     mine = join(plan, [x_mine, y_mine, *far_mine])

time: 169 us -> 168 us (level)
  transfers between devices with their start and end apart: 22 -> 22, of which waited for: 15 -> 15; matrix products, arithmetic and copies ran while one was open for 0% -> 0% of each run, Pallas kernels for 23% -> 24%
where the time goes in v3:
time: 168 us; the launch traced here: 167 us
  Pallas kernels  92.5 us (55%)
  waiting for transfers between devices  42.5 us (25%)
  starting transfers between devices  28.1 us (17%)
  other arithmetic  2.52 us (2%)
    pallas_call x4, Pallas kernels, run_blocks(): pl.pallas_call(kernel, grid_spec=pltpu.PrefetchScalarGridSpec(num_scalar_...  79.8 us
    ppermute x12, waiting for transfers between devices, swap_dp(): return lax.ppermute(block, 'dp', route)  33 us
    ppermute x10, starting transfers between devices, swap_section(): return lax.ppermute(block, 'section', route)  14.7 us
    ppermute x12, starting transfers between devices, swap_dp(): return lax.ppermute(block, 'dp', route)  13.3 us
    ppermute x10, waiting for transfers between devices, swap_section(): return lax.ppermute(block, 'section', route)  9.51 us
    pallas_call x1, Pallas kernels, finish_grads(): pl.pallas_call(functools.partial(grads_kernel, plan, latents.shape[1]), g...  3.99 us
    pallas_call x2, Pallas kernels, spread_weights(): pl.pallas_call(functools.partial(spread_kernel, plan, near), grid_spec=pl...  3.49 us
    pallas_call x1, Pallas kernels, pack_weights(): pl.pallas_call(functools.partial(pack_kernel, plan, latent), in_specs=[pl...  3.37 us
  transfers between devices with their start and end apart: 22, of which 15 were waited for; matrix products, arithmetic and copies ran while one was open for 0% of the time, Pallas kernels for 24%

profile of v3, /device:TPU:0, one launch (start us, length us, event | category | flops | bytes accessed | tf_op | source)
XLA Modules:
  0.0 167.4 jit_solution(16021574274949325103)
XLA Ops:
  0.7 3.4 %shard_map.187 = (bf16[1152,512]{1,0:T(8,128)(2,1)}, bf16[256,512]{1,0:T(8,128)(2,1)}, bf16[576,512]{1,0:T(8,128)(2,1)}, bf16[144,512]{1,0:T(8,128)(2,1)}) custom-call(bf16[771,512]{1,0:T(8,128)(2,1)} %bitcast.15, bf16[1,512]{1,0:T(2,128)(2,1)} %gain_first.1, bf16[1,512]{1,0:T(2,128)(2,1)} %refs_2_.1, bf16[512,512]{1,0:T(8,128)(2,1)} %bitcast.17, ...), custom_call_target="tpu_custom_call" | custom-call | flops 33554432 | bytes 2359296 | tf_op jit(solution)/shard_map/pallas_call | solution.py:449
  4.0 4.0 %collective-permute-start = (bf16[144,512]{1,0:T(8,128)(2,1)}, bf16[144,512]{1,0:T(8,128)(2,1)S(1)}, u32[]{:S(2)}, u32[]{:S(2)}) collective-permute-start(bf16[144,512]{1,0:T(8,128)(2,1)} %get-tuple-element.51), channel_id=1, source_target_pairs={{0,24},{8,16},{16,8},{24,0},{1,25},{9,17},{17,9},{25,1},{2,26},{10... | collective-permute-start | bytes 442376 | tf_op jit(solution)/shard_map/ppermute | solution.py:584
  8.7 4.2 %collective-permute-done.refs_2_ = bf16[144,512]{1,0:T(8,128)(2,1)S(1)} collective-permute-done((bf16[144,512]{1,0:T(8,128)(2,1)}, bf16[144,512]{1,0:T(8,128)(2,1)S(1)}, u32[]{:S(2)}, u32[]{:S(2)}) %collective-permute-start) | collective-permute-done | bytes 147488 | tf_op jit(solution)/shard_map/ppermute | solution.py:584
  12.9 2.0 %collective-permute-start.2 = (bf16[576,512]{1,0:T(8,128)(2,1)}, bf16[576,512]{1,0:T(8,128)(2,1)S(1)}, u32[]{:S(2)}, u32[]{:S(2)}) collective-permute-start(bf16[576,512]{1,0:T(8,128)(2,1)} %get-tuple-element.56), channel_id=1, source_target_pairs={{0,16},{8,24},{16,0},{24,8},{1,17},{9,25},{17,1},{25,9},{2,18},{10... | collective-permute-start | bytes 1769480 | tf_op jit(solution)/shard_map/ppermute | solution.py:584
  16.5 2.6 %collective-permute-start.4 = (bf16[144,512]{1,0:T(8,128)(2,1)S(1)}, bf16[144,512]{1,0:T(8,128)(2,1)S(1)}, u32[]{:S(2)}, u32[]{:S(2)}) collective-permute-start(bf16[144,512]{1,0:T(8,128)(2,1)S(1)} %collective-permute-done.refs_2_), channel_id=1, source_target_pairs={{0,4},{1,5},{2,6},{3,7},{4,0},{5,1},{6,2},{7,3},{8,12},{9,13},{10,... | collective-permute-start | bytes 442376 | tf_op jit(solution)/shard_map/ppermute | solution.py:589
  20.7 7.6 %collective-permute-done.4.refs_4_ = bf16[144,512]{1,0:T(8,128)(2,1)S(1)} collective-permute-done((bf16[144,512]{1,0:T(8,128)(2,1)S(1)}, bf16[144,512]{1,0:T(8,128)(2,1)S(1)}, u32[]{:S(2)}, u32[]{:S(2)}) %collective-permute-start.4) | collective-permute-done | bytes 147488 | tf_op jit(solution)/shard_map/ppermute | solution.py:589
  29.5 1.9 %shard_map.189.refs_0_ = bf16[4,1152,512]{2,1,0:T(8,128)(2,1)S(1)} custom-call(s32[3]{0:T(128)S(1)} %pad_add_fusion.sc, bf16[1152,512]{1,0:T(8,128)(2,1)S(1)} %copy-done.2, bf16[1728,512]{1,0:T(8,128)(2,1)S(1)} %shard_map.188.refs_1_), custom_call_target="tpu_custom_call" | custom-call | bytes 4718592 | tf_op jit(solution)/shard_map/pallas_call | solution.py:510
  34.8 33.0 %shard_map.191 = (bf16[7680,512]{1,0:T(8,128)(2,1)}, bf16[7680,512]{1,0:T(8,128)(2,1)}, bf16[1152,512]{1,0:T(8,128)(2,1)S(1)}, bf16[1152,512]{1,0:T(8,128)(2,1)S...) custom-call(s32[3]{0:T(128)S(1)} %pad_add_fusion.sc, ...), custom_call_target="tpu_custom_call" | custom-call | flops 25367150592 | bytes 14155776 | tf_op jit(solution)/shard_map/pallas_call | solution.py:393
  68.2 23.2 %shard_map.192 = (bf16[7680,512]{1,0:T(8,128)(2,1)}, bf16[7680,512]{1,0:T(8,128)(2,1)}, bf16[768,512]{1,0:T(8,128)(2,1)S(1)}, bf16[768,512]{1,0:T(8,128)(2,1)S(1...) custom-call(s32[3]{0:T(128)S(1)} %pad_add_fusion.sc, ...), custom_call_target="tpu_custom_call", output_to_operand_aliasing={{0}: (10, {}), {1}: (11, {})} | custom-call | flops 16911433728 | bytes 9437184 | tf_op jit(solution)/shard_map/pallas_call | solution.py:393
  91.4 2.7 %collective-permute-start.7 = (bf16[768,512]{1,0:T(8,128)(2,1)S(1)}, bf16[768,512]{1,0:T(8,128)(2,1)S(1)}, u32[]{:S(2)}, u32[]{:S(2)}) collective-permute-start(bf16[768,512]{1,0:T(8,128)(2,1)S(1)} %get-tuple-element.60), channel_id=1, source_target_pairs={{0,8},{8,0},{16,24},{24,16},{1,9},{9,1},{17,25},{25,17},{2,10},{10... | collective-permute-start | bytes 2359304 | tf_op jit(solution)/shard_map/ppermute | solution.py:584
  97.1 13.7 %shard_map.193 = (bf16[7680,512]{1,0:T(8,128)(2,1)}, bf16[7680,512]{1,0:T(8,128)(2,1)}, bf16[576,512]{1,0:T(8,128)(2,1)S(1)}, bf16[576,512]{1,0:T(8,128)(2,1)S(1)}) custom-call(s32[3]{0:T(128)S(1)} %pad_add_fusion.sc, bf16[7680,512]{1,0:T(8,128)(2,1)S(1)} %bitcast.14, bf16[7680,512]{1,0:T(8,128)(2,1)} %g_in.7, ...), custom_call_target="tpu_custom_call", output_to_operand_aliasing={{0}: (10, {}), {1}: (11, {})} | custom-call | flops 9663676416 | bytes 14155776 | tf_op jit(solution)/shard_map/pallas_call | solution.py:393
  110.8 2.0 %collective-permute-done.7.refs_0_ = bf16[768,512]{1,0:T(8,128)(2,1)S(1)} collective-permute-done((bf16[768,512]{1,0:T(8,128)(2,1)S(1)}, bf16[768,512]{1,0:T(8,128)(2,1)S(1)}, u32[]{:S(2)}, u32[]{:S(2)}) %collective-permute-start.7) | collective-permute-done | bytes 786464 | tf_op jit(solution)/shard_map/ppermute | solution.py:584
  112.9 10.0 %shard_map.194 = (bf16[7680,512]{1,0:T(8,128)(2,1)}, bf16[7680,512]{1,0:T(8,128)(2,1)}, bf16[576,512]{1,0:T(8,128)(2,1)S(1)}, bf16[576,512]{1,0:T(8,128)(2,1)S(1)}) custom-call(s32[3]{0:T(128)S(1)} %pad_add_fusion.sc, bf16[7680,512]{1,0:T(8,128)(2,1)S(1)} %bitcast.14, bf16[7680,512]{1,0:T(8,128)(2,1)} %g_in.7, ...), custom_call_target="tpu_custom_call", output_to_operand_aliasing={{0}: (10, {}), {1}: (11, {})} | custom-call | flops 6442450944 | bytes 9437184 | tf_op jit(solution)/shard_map/pallas_call | solution.py:393
  123.7 2.0 %collective-permute-done.11 = bf16[576,512]{1,0:T(8,128)(2,1)S(1)} collective-permute-done((bf16[576,512]{1,0:T(8,128)(2,1)S(1)}, bf16[576,512]{1,0:T(8,128)(2,1)S(1)}, u32[]{:S(2)}, u32[]{:S(2)}) %collective-permute-start.11) | collective-permute-done | bytes 589856 | tf_op jit(solution)/shard_map/ppermute | solution.py:589
  127.3 2.9 %collective-permute-start.12 = (bf16[144,512]{1,0:T(8,128)(2,1)S(1)}, bf16[144,512]{1,0:T(8,128)(2,1)S(1)}, u32[]{:S(2)}, u32[]{:S(2)}) collective-permute-start(bf16[144,512]{1,0:T(8,128)(2,1)S(1)} %get-tuple-element.109), channel_id=1, source_target_pairs={{0,6},{1,7},{2,4},{3,5},{4,2},{5,3},{6,0},{7,1},{8,14},{9,15},{10,... | collective-permute-start | bytes 442376 | tf_op jit(solution)/shard_map/ppermute | solution.py:589
  131.7 4.2 %collective-permute-done.12 = bf16[144,512]{1,0:T(8,128)(2,1)S(1)} collective-permute-done((bf16[144,512]{1,0:T(8,128)(2,1)S(1)}, bf16[144,512]{1,0:T(8,128)(2,1)S(1)}, u32[]{:S(2)}, u32[]{:S(2)}) %collective-permute-start.12) | collective-permute-done | bytes 147488 | tf_op jit(solution)/shard_map/ppermute | solution.py:589
  135.9 8.3 %collective-permute-done.13 = bf16[144,512]{1,0:T(8,128)(2,1)S(1)} collective-permute-done((bf16[144,512]{1,0:T(8,128)(2,1)S(1)}, bf16[144,512]{1,0:T(8,128)(2,1)S(1)}, u32[]{:S(2)}, u32[]{:S(2)}) %collective-permute-start.13) | collective-permute-done | bytes 147488 | tf_op jit(solution)/shard_map/ppermute | solution.py:589
  144.5 3.1 %collective-permute-start.16 = (bf16[144,512]{1,0:T(8,128)(2,1)S(1)}, bf16[144,512]{1,0:T(8,128)(2,1)S(1)}, u32[]{:S(2)}, u32[]{:S(2)}) collective-permute-start(bf16[144,512]{1,0:T(8,128)(2,1)S(1)} %add_convert_fusion.2.refs_0_), channel_id=1, source_target_pairs={{0,4},{1,5},{2,6},{3,7},{4,0},{5,1},{6,2},{7,3},{8,12},{9,13},{10,... | collective-permute-start | bytes 442376 | tf_op jit(solution)/shard_map/ppermute | solution.py:589
  148.8 3.5 %collective-permute-done.15.refs_1_ = bf16[144,512]{1,0:T(8,128)(2,1)S(1)} collective-permute-done((bf16[144,512]{1,0:T(8,128)(2,1)S(1)}, bf16[144,512]{1,0:T(8,128)(2,1)S(1)}, u32[]{:S(2)}, u32[]{:S(2)}) %collective-permute-start.15) | collective-permute-done | bytes 147488 | tf_op jit(solution)/shard_map/ppermute | solution.py:589
  152.5 2.0 %collective-permute-start.18 = (f32[2,256]{1,0:T(2,128)S(1)}, f32[2,256]{1,0:T(2,128)S(1)}, u32[]{:S(2)}, u32[]{:S(2)}) collective-permute-start(f32[2,256]{1,0:T(2,128)S(1)} %get-tuple-element.112), channel_id=1, source_target_pairs={{0,8},{8,0},{16,24},{24,16},{1,9},{9,1},{17,25},{25,17},{2,10},{10... | collective-permute-start | bytes 6152 | tf_op jit(solution)/shard_map/ppermute | solution.py:584
  154.5 1.8 %collective-permute-start.19 = (f32[2,256]{1,0:T(2,128)S(1)}, f32[2,256]{1,0:T(2,128)S(1)}, u32[]{:S(2)}, u32[]{:S(2)}) collective-permute-start(f32[2,256]{1,0:T(2,128)S(1)} %get-tuple-element.114), channel_id=1, source_target_pairs={{0,16},{8,24},{16,0},{24,8},{1,17},{9,25},{17,1},{25,9},{2,18},{10... | collective-permute-start | bytes 6152 | tf_op jit(solution)/shard_map/ppermute | solution.py:584
  156.3 2.3 %collective-permute-done.16.refs_2_ = bf16[144,512]{1,0:T(8,128)(2,1)S(1)} collective-permute-done((bf16[144,512]{1,0:T(8,128)(2,1)S(1)}, bf16[144,512]{1,0:T(8,128)(2,1)S(1)}, u32[]{:S(2)}, u32[]{:S(2)}) %collective-permute-start.16) | collective-permute-done | bytes 147488 | tf_op jit(solution)/shard_map/ppermute | solution.py:589
  161.4 2.0 %collective-permute-done.21.other = bf16[576,512]{1,0:T(8,128)(2,1)S(1)} collective-permute-done((bf16[576,512]{1,0:T(8,128)(2,1)S(1)}, bf16[576,512]{1,0:T(8,128)(2,1)S(1)}, u32[]{:S(2)}, u32[]{:S(2)}) %collective-permute-start.21) | collective-permute-done | bytes 589856 | tf_op jit(solution)/shard_map/ppermute | solution.py:589
  163.4 4.0 %shard_map.196 = (f32[771,4,128]{2,1,0:T(4,128)}, f32[1,512]{1,0:T(1,128)}, f32[1,512]{1,0:T(1,128)}, f32[512,512]{1,0:T(8,128)}, f32[1,512]{1,0:T(1,128)}, /*index=5*/f32[1,512]{1,0:T(1,128)}) custom-call(s32[3]{0:T(128)S(1)} %pad_add_fusion.sc, bf16[576,512]{1,0:T(8,128)(2,1)S(1)} %shard_map.195.mine, bf16[576,512]{1,0:T(8,128)(2,1)S(1)} %collective-permute-done.21.other, ...), custom_call_target="tpu_custom_call" | custom-call | flops 33554432 | bytes 4718592 | tf_op jit(solution)/shard_map/pallas_call | solution.py:569
  (66 shorter events, 20.2 us)
Async XLA Ops:
  4.0 8.8 %collective-permute-start = (bf16[144,512]{1,0:T(8,128)(2,1)}, bf16[144,512]{1,0:T(8,128)(2,1)S(1)}, u32[]{:S(2)}, u32[]{:S(2)}) collective-permute-start(bf16[144,512]{1,0:T(8,128)(2,1)} %get-tuple-element.51), channel_id=1, source_target_pairs={{0,24},{8,16},{16,8},{24,0},{1,25},{9,17},{17,9},{25,1},{2,26},{10... | collective-permute-start | bytes 442376 | tf_op jit(solution)/shard_map/ppermute | solution.py:584
  8.0 20.3 %collective-permute-start.1 = (bf16[576,512]{1,0:T(8,128)(2,1)}, bf16[576,512]{1,0:T(8,128)(2,1)S(1)}, u32[]{:S(2)}, u32[]{:S(2)}) collective-permute-start(bf16[576,512]{1,0:T(8,128)(2,1)} %get-tuple-element.56), channel_id=1, source_target_pairs={{0,8},{8,0},{16,24},{24,16},{1,9},{9,1},{17,25},{25,17},{2,10},{10... | collective-permute-start | bytes 1769480 | tf_op jit(solution)/shard_map/ppermute | solution.py:584
  12.9 15.4 %collective-permute-start.2 = (bf16[576,512]{1,0:T(8,128)(2,1)}, bf16[576,512]{1,0:T(8,128)(2,1)S(1)}, u32[]{:S(2)}, u32[]{:S(2)}) collective-permute-start(bf16[576,512]{1,0:T(8,128)(2,1)} %get-tuple-element.56), channel_id=1, source_target_pairs={{0,16},{8,24},{16,0},{24,8},{1,17},{9,25},{17,1},{25,9},{2,18},{10... | collective-permute-start | bytes 1769480 | tf_op jit(solution)/shard_map/ppermute | solution.py:584
  14.9 5.8 %collective-permute-start.3 = (bf16[144,512]{1,0:T(8,128)(2,1)S(1)}, bf16[144,512]{1,0:T(8,128)(2,1)S(1)}, u32[]{:S(2)}, u32[]{:S(2)}) collective-permute-start(bf16[144,512]{1,0:T(8,128)(2,1)S(1)} %collective-permute-done.refs_2_), channel_id=1, source_target_pairs={{0,2},{1,3},{2,0},{3,1},{4,6},{5,7},{6,4},{7,5},{8,10},{9,11},{10,... | collective-permute-start | bytes 442376 | tf_op jit(solution)/shard_map/ppermute | solution.py:589
  16.5 11.8 %collective-permute-start.4 = (bf16[144,512]{1,0:T(8,128)(2,1)S(1)}, bf16[144,512]{1,0:T(8,128)(2,1)S(1)}, u32[]{:S(2)}, u32[]{:S(2)}) collective-permute-start(bf16[144,512]{1,0:T(8,128)(2,1)S(1)} %collective-permute-done.refs_2_), channel_id=1, source_target_pairs={{0,4},{1,5},{2,6},{3,7},{4,0},{5,1},{6,2},{7,3},{8,12},{9,13},{10,... | collective-permute-start | bytes 442376 | tf_op jit(solution)/shard_map/ppermute | solution.py:589
  19.1 9.2 %collective-permute-start.5 = (bf16[144,512]{1,0:T(8,128)(2,1)S(1)}, bf16[144,512]{1,0:T(8,128)(2,1)S(1)}, u32[]{:S(2)}, u32[]{:S(2)}) collective-permute-start(bf16[144,512]{1,0:T(8,128)(2,1)S(1)} %collective-permute-done.refs_2_), channel_id=1, source_target_pairs={{0,6},{1,7},{2,4},{3,5},{4,2},{5,3},{6,0},{7,1},{8,14},{9,15},{10,... | collective-permute-start | bytes 442376 | tf_op jit(solution)/shard_map/ppermute | solution.py:589
  29.4 3.8 %collective-permute-start.6 = (bf16[1728,512]{1,0:T(8,128)(2,1)S(1)}, bf16[1728,512]{1,0:T(8,128)(2,1)S(1)}, u32[]{:S(2)}, u32[]{:S(2)}) collective-permute-start(bf16[1728,512]{1,0:T(8,128)(2,1)S(1)} %shard_map.188.refs_1_), channel_id=1, source_target_pairs={{0,1},{1,0},{2,3},{3,2},{4,5},{5,4},{6,7},{7,6},{8,9},{9,8},{10,11... | collective-permute-start | bytes 5308424 | tf_op jit(solution)/shard_map/ppermute | solution.py:589
  67.8 28.0 %collective-permute-start.10 = (bf16[1152,512]{1,0:T(8,128)(2,1)S(1)}, bf16[1152,512]{1,0:T(8,128)(2,1)S(1)}, u32[]{:S(2)}, u32[]{:S(2)}) collective-permute-start(bf16[1152,512]{1,0:T(8,128)(2,1)S(1)} %get-tuple-element.64), channel_id=1, source_target_pairs={{0,16},{8,24},{16,0},{24,8},{1,17},{9,25},{17,1},{25,9},{2,18},{10... | collective-permute-start | bytes 3538952 | tf_op jit(solution)/shard_map/ppermute | solution.py:584
  68.2 28.8 %collective-permute-start.9 = (bf16[1152,512]{1,0:T(8,128)(2,1)S(1)}, bf16[1152,512]{1,0:T(8,128)(2,1)S(1)}, u32[]{:S(2)}, u32[]{:S(2)}) collective-permute-start(bf16[1152,512]{1,0:T(8,128)(2,1)S(1)} %get-tuple-element.63), channel_id=1, source_target_pairs={{0,8},{8,0},{16,24},{24,16},{1,9},{9,1},{17,25},{25,17},{2,10},{10... | collective-permute-start | bytes 3538952 | tf_op jit(solution)/shard_map/ppermute | solution.py:584
  91.4 21.4 %collective-permute-start.7 = (bf16[768,512]{1,0:T(8,128)(2,1)S(1)}, bf16[768,512]{1,0:T(8,128)(2,1)S(1)}, u32[]{:S(2)}, u32[]{:S(2)}) collective-permute-start(bf16[768,512]{1,0:T(8,128)(2,1)S(1)} %get-tuple-element.60), channel_id=1, source_target_pairs={{0,8},{8,0},{16,24},{24,16},{1,9},{9,1},{17,25},{25,17},{2,10},{10... | collective-permute-start | bytes 2359304 | tf_op jit(solution)/shard_map/ppermute | solution.py:584
  94.1 18.8 %collective-permute-start.8 = (bf16[768,512]{1,0:T(8,128)(2,1)S(1)}, bf16[768,512]{1,0:T(8,128)(2,1)S(1)}, u32[]{:S(2)}, u32[]{:S(2)}) collective-permute-start(bf16[768,512]{1,0:T(8,128)(2,1)S(1)} %get-tuple-element.61), channel_id=1, source_target_pairs={{0,16},{8,24},{16,0},{24,8},{1,17},{9,25},{17,1},{25,9},{2,18},{10... | collective-permute-start | bytes 2359304 | tf_op jit(solution)/shard_map/ppermute | solution.py:584
  123.7 2.0 %collective-permute-start.11 = (bf16[576,512]{1,0:T(8,128)(2,1)S(1)}, bf16[576,512]{1,0:T(8,128)(2,1)S(1)}, u32[]{:S(2)}, u32[]{:S(2)}) collective-permute-start(bf16[576,512]{1,0:T(8,128)(2,1)S(1)} %add_convert_fusion.1), channel_id=1, source_target_pairs={{0,1},{1,0},{2,3},{3,2},{4,5},{5,4},{6,7},{7,6},{8,9},{9,8},{10,11... | collective-permute-start | bytes 1769480 | tf_op jit(solution)/shard_map/ppermute | solution.py:589
  127.2 36.2 %copy-start = (bf16[1,771,512]{2,1,0:T(8,128)(2,1)S(1)}, bf16[1,771,512]{2,1,0:T(8,128)(2,1)}, u32[]{:S(2)}) copy-start(bf16[1,771,512]{2,1,0:T(8,128)(2,1)} %param.17) | copy-start | bytes 2368516
  127.2 36.2 %copy-start.1 = (bf16[1,512,512]{2,1,0:T(8,128)(2,1)S(1)}, bf16[1,512,512]{2,1,0:T(8,128)(2,1)}, u32[]{:S(2)}) copy-start(bf16[1,512,512]{2,1,0:T(8,128)(2,1)} %param.20) | copy-start | bytes 1572868
  127.3 8.7 %collective-permute-start.12 = (bf16[144,512]{1,0:T(8,128)(2,1)S(1)}, bf16[144,512]{1,0:T(8,128)(2,1)S(1)}, u32[]{:S(2)}, u32[]{:S(2)}) collective-permute-start(bf16[144,512]{1,0:T(8,128)(2,1)S(1)} %get-tuple-element.109), channel_id=1, source_target_pairs={{0,6},{1,7},{2,4},{3,5},{4,2},{5,3},{6,0},{7,1},{8,14},{9,15},{10,... | collective-permute-start | bytes 442376 | tf_op jit(solution)/shard_map/ppermute | solution.py:589
  130.2 14.1 %collective-permute-start.13 = (bf16[144,512]{1,0:T(8,128)(2,1)S(1)}, bf16[144,512]{1,0:T(8,128)(2,1)S(1)}, u32[]{:S(2)}, u32[]{:S(2)}) collective-permute-start(bf16[144,512]{1,0:T(8,128)(2,1)S(1)} %get-tuple-element.111), channel_id=1, source_target_pairs={{0,4},{1,5},{2,6},{3,7},{4,0},{5,1},{6,2},{7,3},{8,12},{9,13},{10,... | collective-permute-start | bytes 442376 | tf_op jit(solution)/shard_map/ppermute | solution.py:589
  130.9 13.3 %collective-permute-start.14 = (bf16[144,512]{1,0:T(8,128)(2,1)S(1)}, bf16[144,512]{1,0:T(8,128)(2,1)S(1)}, u32[]{:S(2)}, u32[]{:S(2)}) collective-permute-start(bf16[144,512]{1,0:T(8,128)(2,1)S(1)} %get-tuple-element.110), channel_id=1, source_target_pairs={{0,2},{1,3},{2,0},{3,1},{4,6},{5,7},{6,4},{7,5},{8,10},{9,11},{10,... | collective-permute-start | bytes 442376 | tf_op jit(solution)/shard_map/ppermute | solution.py:589
  144.4 7.9 %collective-permute-start.15 = (bf16[144,512]{1,0:T(8,128)(2,1)S(1)}, bf16[144,512]{1,0:T(8,128)(2,1)S(1)}, u32[]{:S(2)}, u32[]{:S(2)}) collective-permute-start(bf16[144,512]{1,0:T(8,128)(2,1)S(1)} %add_convert_fusion.2.refs_0_), channel_id=1, source_target_pairs={{0,2},{1,3},{2,0},{3,1},{4,6},{5,7},{6,4},{7,5},{8,10},{9,11},{10,... | collective-permute-start | bytes 442376 | tf_op jit(solution)/shard_map/ppermute | solution.py:589
  144.5 14.1 %collective-permute-start.16 = (bf16[144,512]{1,0:T(8,128)(2,1)S(1)}, bf16[144,512]{1,0:T(8,128)(2,1)S(1)}, u32[]{:S(2)}, u32[]{:S(2)}) collective-permute-start(bf16[144,512]{1,0:T(8,128)(2,1)S(1)} %add_convert_fusion.2.refs_0_), channel_id=1, source_target_pairs={{0,4},{1,5},{2,6},{3,7},{4,0},{5,1},{6,2},{7,3},{8,12},{9,13},{10,... | collective-permute-start | bytes 442376 | tf_op jit(solution)/shard_map/ppermute | solution.py:589
  147.5 11.1 %collective-permute-start.17 = (bf16[144,512]{1,0:T(8,128)(2,1)S(1)}, bf16[144,512]{1,0:T(8,128)(2,1)S(1)}, u32[]{:S(2)}, u32[]{:S(2)}) collective-permute-start(bf16[144,512]{1,0:T(8,128)(2,1)S(1)} %add_convert_fusion.2.refs_0_), channel_id=1, source_target_pairs={{0,6},{1,7},{2,4},{3,5},{4,2},{5,3},{6,0},{7,1},{8,14},{9,15},{10,... | collective-permute-start | bytes 442376 | tf_op jit(solution)/shard_map/ppermute | solution.py:589
  152.5 6.9 %collective-permute-start.18 = (f32[2,256]{1,0:T(2,128)S(1)}, f32[2,256]{1,0:T(2,128)S(1)}, u32[]{:S(2)}, u32[]{:S(2)}) collective-permute-start(f32[2,256]{1,0:T(2,128)S(1)} %get-tuple-element.112), channel_id=1, source_target_pairs={{0,8},{8,0},{16,24},{24,16},{1,9},{9,1},{17,25},{25,17},{2,10},{10... | collective-permute-start | bytes 6152 | tf_op jit(solution)/shard_map/ppermute | solution.py:584
  154.5 4.9 %collective-permute-start.19 = (f32[2,256]{1,0:T(2,128)S(1)}, f32[2,256]{1,0:T(2,128)S(1)}, u32[]{:S(2)}, u32[]{:S(2)}) collective-permute-start(f32[2,256]{1,0:T(2,128)S(1)} %get-tuple-element.114), channel_id=1, source_target_pairs={{0,16},{8,24},{16,0},{24,8},{1,17},{9,25},{17,1},{25,9},{2,18},{10... | collective-permute-start | bytes 6152 | tf_op jit(solution)/shard_map/ppermute | solution.py:584
  156.3 4.5 %collective-permute-start.20 = (f32[2,256]{1,0:T(2,128)S(1)}, f32[2,256]{1,0:T(2,128)S(1)}, u32[]{:S(2)}, u32[]{:S(2)}) collective-permute-start(f32[2,256]{1,0:T(2,128)S(1)} %get-tuple-element.113), channel_id=1, source_target_pairs={{0,24},{8,16},{16,8},{24,0},{1,25},{9,17},{17,9},{25,1},{2,26},{10... | collective-permute-start | bytes 6152 | tf_op jit(solution)/shard_map/ppermute | solution.py:584
  161.4 2.0 %collective-permute-start.21 = (bf16[576,512]{1,0:T(8,128)(2,1)S(1)}, bf16[576,512]{1,0:T(8,128)(2,1)S(1)}, u32[]{:S(2)}, u32[]{:S(2)}) collective-permute-start(bf16[576,512]{1,0:T(8,128)(2,1)S(1)} %shard_map.195.mine), channel_id=1, source_target_pairs={{0,1},{1,0},{2,3},{3,2},{4,5},{5,4},{6,7},{7,6},{8,9},{9,8},{10,11... | collective-permute-start | bytes 1769480 | tf_op jit(solution)/shard_map/ppermute | solution.py:589
  (11 other events, 174.4 us)
